TPU v7x, 1024 devices: a whole 4x4x32 slice. The times are simulated.
1024 devices in a mesh: dp: 64 (over z, core), tensor: 16 (over x, y).
Axes of the slice: x: 4, y: 4, z: 32, core: 2. Of those that a mesh axis runs over, the one named last changes fastest.
Arguments:
- cotan: bfloat16 [8192, 4096], P(('dp', 'tensor')), may hold values from -6 to 6
- gate_pre: bfloat16 [8192, 14336], P('dp', 'tensor'), may hold values from -6 to 6
- up_pre: bfloat16 [8192, 14336], P('dp', 'tensor'), may hold values from -6 to 6
- tiles: bfloat16 [3072, 128, 128], P(('dp', 'tensor')), as said below
- tile_block: int32 [3072], P(('dp', 'tensor')), may hold values from -1 to 3583, as said below
Outputs:
- dgate: bfloat16 [8192, 14336], P('dp', 'tensor')
- dup: bfloat16 [8192, 14336], P('dp', 'tensor')
- tile_grad: float32 [3072, 128, 128], P(('dp', 'tensor'))
Inputs may be any that keep to these rules, and one draw needn't show every extreme that they name: tile_block[s] is c * 32 + r for block (c, r) of w_down, or -1 for an empty slot. Every hidden block c has exactly 16 nonzero blocks, each named by exactly one slot; the slots of the device at index j of tensor name only blocks with j * 7 <= c < (j + 1) * 7, and for every index of tensor some owner has all of its 3 slots used. `tiles`: slots with tile_block -1 hold zeros.
All inputs are finite; a program needn't handle non-finite values.
Results may differ from a plain program's by a relative error of at most 0.0029.
Values may be sent and summed in bfloat16 or wider, within the bound.
No kernel may reach another device: no remote copies, remote signals or barrier semaphores. Data moves between devices by JAX's collectives and lax.ppermute only.
A program may use at most 64 MiB of HBM per device.

v0:
```python
import math

import jax
import jax.numpy as jnp
from jax import lax
from jax.sharding import PartitionSpec as P


def slot_tables(codes, rows_b, cols_b, first):
    valid = codes >= 0
    safe = jnp.maximum(codes, 0)
    column = safe // rows_b - first
    row_blk = safe % rows_b
    col_hot = (jnp.arange(cols_b, dtype=jnp.int32)[None, :] == column[:, None]) & valid[:, None]
    row_hot = (jnp.arange(rows_b, dtype=jnp.int32)[None, :] == row_blk[:, None]) & valid[:, None]
    return (col_hot, row_hot)


def add_slots(dhid, cot_three, piece_tiles, piece_codes, first):
    rows_b = cot_three.shape[1]
    side = cot_three.shape[2]
    cols_b = dhid.shape[1]
    count = piece_tiles.shape[0]
    groups = math.gcd(count, 8)
    tiles_g = piece_tiles.reshape(groups, count // groups, side, side)
    codes_g = piece_codes.reshape(groups, count // groups)

    def one_group(total, pair):
        tile_set, code_set = pair
        col_hot, row_hot = slot_tables(code_set, rows_b, cols_b, first)
        cot_cols = jnp.einsum(
            "trk,pr->tpk",
            cot_three,
            row_hot.astype(jnp.bfloat16),
            preferred_element_type=jnp.float32,
        ).astype(jnp.bfloat16)
        contrib = jnp.einsum("tpk,pjk->tpj", cot_cols, tile_set, preferred_element_type=jnp.float32)
        placed = jnp.einsum(
            "tpj,pc->tcj", contrib, col_hot.astype(jnp.float32), precision=lax.Precision.HIGHEST
        )
        return (total + placed, None)

    total, _ = lax.scan(one_group, dhid, (tiles_g, codes_g))
    return total


def local(cotan, gate_pre, up_pre, tiles, tile_block):
    side = tiles.shape[1]
    width = cotan.shape[1]
    rows_b = width // side
    hid_dev = gate_pre.shape[1]
    cols_b = hid_dev // side
    owners = lax.axis_size("dp")
    first = lax.axis_index("tensor") * cols_b
    group = lax.all_gather(cotan, "tensor", axis=0, tiled=True)
    tokens_n = group.shape[0]
    cot_three = group.reshape(tokens_n, rows_b, side)
    start_sum = jnp.zeros((tokens_n, cols_b, side), jnp.float32)
    gathered, codes_all = (
        lax.all_gather(tiles, "dp", axis=0, tiled=True),
        lax.all_gather(tile_block, "dp", axis=0, tiled=True),
    )
    dhid = add_slots(start_sum, cot_three, gathered, codes_all, first)
    dhid = dhid.reshape(tokens_n, hid_dev)
    gate = gate_pre.astype(jnp.float32)
    upper = up_pre.astype(jnp.float32)
    sigma = jax.nn.sigmoid(gate)
    silu_g = gate * sigma
    hidden = (silu_g * upper).astype(jnp.bfloat16)
    dgate = (dhid * upper * sigma * (1.0 + gate * (1.0 - sigma))).astype(jnp.bfloat16)
    dup = (dhid * silu_g).astype(jnp.bfloat16)
    hidden_three = hidden.reshape(tokens_n, cols_b, side)
    factor = 1.0 / math.sqrt(tokens_n * owners)
    col_hot, row_hot = slot_tables(codes_all, rows_b, cols_b, first)
    hid_cols = jnp.einsum(
        "tcj,pc->tpj",
        hidden_three,
        col_hot.astype(jnp.bfloat16),
        preferred_element_type=jnp.float32,
    ).astype(jnp.bfloat16)
    cot_cols = jnp.einsum(
        "trk,pr->tpk", cot_three, row_hot.astype(jnp.bfloat16), preferred_element_type=jnp.float32
    ).astype(jnp.bfloat16)
    term = jnp.einsum("tpj,tpk->pjk", hid_cols, cot_cols, preferred_element_type=jnp.float32)
    tile_grad = lax.psum_scatter(term * factor, "dp", scatter_dimension=0, tiled=True)
    return (dgate, dup, tile_grad)


def solution(mesh):
    placed = (
        P(("dp", "tensor"), None),
        P("dp", "tensor"),
        P("dp", "tensor"),
        P(("dp", "tensor"), None, None),
        P(("dp", "tensor")),
    )
    return jax.shard_map(
        local,
        mesh=mesh,
        in_specs=placed,
        out_specs=(P("dp", "tensor"), P("dp", "tensor"), P(("dp", "tensor"), None, None)),
        check_vma=False,
    )
```

profile of v0, /device:TPU:6, one launch (start us, length us, event | category | flops | bytes accessed | tf_op | source)
XLA Modules:
  0.0 542.6 jit_solution(10675179586668093461)
XLA Ops:
  7.2 0.0 all-gather.5.cloned.1.call-start
  7.2 0.7 all-gather.5.cloned.1.call-update
  7.9 0.0 all-gather.3.cloned.1.call-start
  7.9 0.7 all-gather.3.cloned.1.call-update
  8.6 0.0 reduce-scatter.2.cloned.1.call-start
  8.7 1.3 dynamic-slice
  10.7 0.9 dynamic-update-slice
  11.5 46.0 %all-reduce = s32[192]{0:T(256)S(1)} all-reduce(s32[192]{0:T(256)S(1)} %dynamic-update-slice), channel_id=1, replica_groups=mesh['dp'=64,'tensor'=16] {'dp'}, use_global_device_ids=true, to_apply=%add | all-reduce | flops 192 | bytes 1536
  57.5 0.1 reshape.72
  57.5 1.1 copy.17
  58.7 1.8 copy.16
  60.4 37.3 %all-gather.5.cloned.1.call-done = bf16[128,4096]{1,0:T(8,128)(2,1)} async-done(((bf16[8,4096]{1,0:T(8,128)(2,1)}), bf16[128,4096]{1,0:T(8,128)(2,1)}) %all-gather.5.cloned.1.call-update) | async-done | bytes 1048592 | tf_op jit(solution)/shard_map/all_gather | solution.py:55
  97.8 2.4 copy.23
  100.2 5.7 %convert_bitcast_fusion = bf16[128,192,128]{2,1,0:T(8,128)(2,1)} fusion(bf16[128,32,128]{2,1,0:T(8,128)(2,1)} %bitcast.19, s32[192]{0:T(256)S(1)} %get-tuple-element.129, pred[192]{0:T(512)(128)(4,1)S(1)} %broadcast_compare_fusion), kind=kOutput, calls=%fused_computation.29 | convolution fusion | flops 204484608 | bytes 7340992 | tf_op jit(solution)/shard_map/trk,pr->tpk/dot_general | solution.py:81
  105.9 136.5 %all-gather.3.cloned.1.call-done = bf16[192,128,128]{2,1,0:T(8,128)(2,1)} async-done(((bf16[3,128,128]{2,1,0:T(8,128)(2,1)}), bf16[192,128,128]{2,1,0:T(8,128)(2,1)}) %all-gather.3.cloned.1.call-update) | async-done | bytes 6291472 | tf_op jit(solution)/shard_map/all_gather | solution.py:60
  242.3 51.6 %while.13 = (s32[]{:T(128)}, f32[128,7,128]{2,1,0:T(8,128)}, s32[8,24]{1,0:T(8,128)S(1)}, s32[]{:T(128)}, bf16[8,24,128,128]{3,2,1,0:T(8,128)(2,1)}, /*index=5*/bf16[128,32,128]{2,1,0:T(8,128)(2,1)}, s32[]{:T(128)}, s32[]{:T(128)}) while((s32[]{:T(128)}, f32[128,7,128]{2,1,0:T(8,128)}, s32[8,24]{1,0:T(8,128)S(1)}, s32[]{:T(128)}, ...), condition=%wide.region_1.2_spmd.clone, body=%wide.region_0.1_spmd.clone.sunk | while | flops 159484096 | bytes 10617599 | solution.py:43
  242.4 1.6 fusion.65
  244.0 1.8 convolution_bitcast_fusion.3
  245.8 0.6 copy.37
  246.4 1.5 fusion.66
  247.9 1.6 fusion.65
  249.6 1.8 convolution_bitcast_fusion.3
  251.4 0.6 copy.37
  251.9 2.5 fusion.66
  254.5 1.6 fusion.65
  256.1 1.8 convolution_bitcast_fusion.3
  257.9 0.6 copy.37
  258.5 2.5 fusion.66
  261.1 1.6 fusion.65
  262.7 1.8 convolution_bitcast_fusion.3
  264.5 0.6 copy.37
  265.1 2.5 fusion.66
  267.7 1.6 fusion.65
  269.3 1.8 convolution_bitcast_fusion.3
  271.1 0.6 copy.37
  271.7 2.5 fusion.66
  274.2 1.6 fusion.65
  275.9 1.8 convolution_bitcast_fusion.3
  277.7 0.6 copy.37
  278.3 2.5 fusion.66
  280.8 1.6 fusion.65
  282.5 1.8 convolution_bitcast_fusion.3
  284.3 0.6 copy.37
  284.9 2.5 fusion.66
  287.4 1.6 fusion.65
  289.1 1.8 convolution_bitcast_fusion.3
  290.9 0.6 copy.37
  291.4 2.5 fusion.66
  294.0 1.2 copy.15
  295.2 2.0 fusion.33
  297.2 0.2 copy.18
  297.4 1.9 convert_bitcast_fusion.1
  299.3 16.2 %broadcast_multiply_fusion = f32[192,128,128]{2,1,0:T(8,128)} fusion(bf16[128,192,128]{2,1,0:T(8,128)(2,1)} %convert_bitcast_fusion, bf16[128,192,128]{2,1,0:T(8,128)(2,1)S(1)} %convert_bitcast_fusion.1), kind=kOutput, calls=%fused_computation.28 | convolution fusion | flops 808452096 | bytes 25165824 | tf_op jit(solution)/shard_map/tpj,tpk->pjk/dot_general | solution.py:84
  315.6 0.0 copy-start.1
  315.6 0.0 copy-start
  315.6 0.0 reduce-scatter.2.cloned.1.call-update
  315.6 0.9 copy-done.1
  316.5 0.8 copy.22
  317.3 0.0 copy-done
  317.3 0.8 copy.21
  318.2 217.9 %reduce-scatter.2.cloned.1.call-done = f32[3,128,128]{2,1,0:T(8,128)} async-done(((f32[192,128,128]{2,1,0:T(8,128)}), f32[3,128,128]{2,1,0:T(8,128)}) %reduce-scatter.2.cloned.1.call-update) | async-done | bytes 196624 | tf_op jit(solution)/shard_map/reduce_scatter | solution.py:85
  (20 shorter events, 0.2 us)
Async XLA Ops:
  7.2 90.6 %all-gather.5.cloned.1.call-start = ((), (), s32[]{:S(2)}) async-start(), calls=%async_computation.2 | async-start | bytes 1114112 | tf_op jit(solution)/shard_map/all_gather | solution.py:55
  7.9 234.4 %all-gather.3.cloned.1.call-start = ((), (), s32[]{:S(2)}) async-start(), calls=%async_computation.1 | async-start | bytes 6389760 | tf_op jit(solution)/shard_map/all_gather | solution.py:60
  8.6 527.4 %reduce-scatter.2.cloned.1.call-start = ((), (), s32[]{:S(2)}) async-start(), calls=%async_computation.3 | async-start | bytes 12779520 | tf_op jit(solution)/shard_map/reduce_scatter | solution.py:85
  315.6 0.9 copy-start.1
  315.6 1.8 copy-start
Sparse Core Ops, SparseCore 0:
  12.2 85.5 all-gather.4
  100.5 141.8 all-gather.2
  315.7 220.3 reduce-scatter.1
where the time goes:
time: 544 us; the launch traced here: 543 us
  waiting for transfers between devices  393 us (72%)
  matrix products  70.6 us (13%)
  blocking collectives  46 us (8%)
  local copies, waits for them, and re-layouts  16 us (3%)
  between operations  14.5 us (3%)
    reduce_scatter x1, waiting for transfers between devices, local(): lax.psum_scatter(term * factor, 'dp', scatter_dimension=0, tiled=True)  218 us
    all_gather x1, waiting for transfers between devices, local(): lax.all_gather(tiles, 'dp', axis=0, tiled=True)  136 us
    unnamed x1, blocking collectives  46 us
    all_gather x1, waiting for transfers between devices, local(): group = lax.all_gather(cotan, 'tensor', axis=0, tiled=True)  37.3 us
    dot_general x8, matrix products, one_group(): jnp.einsum('tpj,pc->tcj', contrib, col_hot.astype(jnp.float32), precision...  19.2 us
    dot_general x1, matrix products, local(): jnp.einsum('tpj,tpk->pjk', hid_cols, cot_cols, preferred_element_type=jnp...  16.2 us
    dot_general x8, matrix products, one_group(): jnp.einsum('tpk,pjk->tpj', cot_cols, tile_set, preferred_element_type=jnp...  14.5 us
    dot_general x8, matrix products, one_group(): jnp.einsum('trk,pr->tpk', cot_three, row_hot.astype(jnp.bfloat16), prefer...  13.2 us
  transfers between devices with their start and end apart: 3, of which 3 were waited for; matrix products, arithmetic and copies ran while one was open for 3% of the time, Pallas kernels for 0%

commit v1 on v0

v1 whole, which is shorter than its diff:
```python
import functools
import math

import jax
import jax.numpy as jnp
from jax import lax
from jax.experimental import pallas as pl
from jax.experimental.pallas import tpu as pltpu
from jax.sharding import PartitionSpec as P

CORES = 2


def grad_kernel(owners, slots, rows_b, factor, place, codes, hid_a, hid_b, cot_a, cot_b,
                low1, high1, low2, high2, kept, hid, cot, dense):
    tokens = cot_a.shape[0]
    side = kept.shape[1]
    half = side // 2
    hid[:, :tokens] = hid_a[...]
    hid[:, tokens:] = hid_b[...]
    cot[:tokens, :] = cot_a[...]
    cot[tokens:, :] = cot_b[...]
    step = 4 * side if rows_b % 4 == 0 else side

    @pl.loop(0, rows_b * side // step)
    def _(n):
        cols = pl.ds(pl.multiple_of(n * step, side), step)
        dense[:, cols] = jnp.dot(hid[...], cot[:, cols], preferred_element_type=jnp.float32) * factor

    z = place[0]
    first = place[1]

    def block(shift, k, i, top, rows):
        owner = lax.rem(z + shift - 4 * k + 2 * owners, owners)
        code = codes[owner * slots + i]
        safe = jnp.maximum(code, first * rows_b)
        column = safe // rows_b - first
        row = lax.rem(safe, rows_b)
        value = dense[
            pl.ds(pl.multiple_of(column * side + top, half), rows),
            pl.ds(pl.multiple_of(row * side, side), side),
        ]
        return jnp.where(code >= 0, value, 0.0)

    @pl.loop(0, owners // 4)
    def _(k):
        for i in range(slots):
            at = k * slots + i
            low1[at] = block(-1, k, i, 0, side).astype(low1.dtype)
            high1[at] = block(1, k, i, 0, side).astype(high1.dtype)
            low2[at] = block(-2, k, i, 0, half).astype(low2.dtype)
            high2[at] = block(2, k, i, half, half).astype(high2.dtype)
            kept[at] = block(0, k, i, 0, side)


def token_kernel(owners, slots, rows_b, place, codes, codes_far, tiles, cot, gate_ref, up_ref,
                 dgate, dup, dense):
    side = tiles.shape[1]
    first = place[1]
    core = place[2]
    dense[...] = jnp.zeros_like(dense)

    def put(code, at):
        @pl.when(code >= 0)
        def _():
            column = code // rows_b - first
            row = lax.rem(code, rows_b)
            dense[
                pl.ds(pl.multiple_of(column * side, side), side),
                pl.ds(pl.multiple_of(row * side, side), side),
            ] = tiles[at]

    @pl.loop(0, owners)
    def _(z):
        for i in range(slots):
            put(codes[z * slots + i], (z * CORES + core) * slots + i)
            put(codes_far[z * slots + i], (z * CORES + 1 - core) * slots + i)

    @pl.loop(0, dense.shape[0] // side)
    def _(n):
        cols = pl.ds(pl.multiple_of(n * side, side), side)
        dhid = lax.dot_general(
            cot[...], dense[cols, :], (((1,), (1,)), ((), ())), preferred_element_type=jnp.float32
        )
        gate = gate_ref[:, cols].astype(jnp.float32)
        upper = up_ref[:, cols].astype(jnp.float32)
        sigma = jax.nn.sigmoid(gate)
        dgate[:, cols] = (dhid * upper * sigma * (1.0 + gate * (1.0 - sigma))).astype(dgate.dtype)
        dup[:, cols] = (dhid * (gate * sigma)).astype(dup.dtype)


def shift_z(value, by, owners):
    pairs = [
        (z * CORES + c, (z + by) % owners * CORES + c) for z in range(owners) for c in range(CORES)
    ]
    return lax.ppermute(value, "dp", pairs)


def swap_core(value, owners):
    pairs = [(z * CORES + c, z * CORES + 1 - c) for z in range(owners) for c in range(CORES)]
    return lax.ppermute(value, "dp", pairs)


def local(cotan, gate_pre, up_pre, tiles, tile_block):
    slots, side, _ = tiles.shape
    tok_dev, width = cotan.shape
    rows_b = width // side
    hid_dev = gate_pre.shape[1]
    cols_b = hid_dev // side
    owners = lax.axis_size("dp") // CORES
    members = lax.axis_size("tensor")
    tokens_n = tok_dev * members
    f32, bf16 = jnp.float32, jnp.bfloat16
    me = lax.axis_index("dp")
    core = me % CORES
    first = lax.axis_index("tensor") * cols_b
    place = jnp.stack([me // CORES, first, core]).astype(jnp.int32)

    gathered = lax.all_gather(tiles, "dp", axis=0, tiled=True)

    own = jnp.zeros((1, 1, 128), jnp.int32).at[0, 0, :slots].set(tile_block)
    rings = [[z * CORES + c for z in range(owners)] for c in range(CORES)]
    table = lax.all_to_all(
        jnp.broadcast_to(own, (owners, 1, 128)), "dp", 0, 0, tiled=True, axis_index_groups=rings
    )
    table_far = swap_core(table, owners)
    codes = table[:, 0, :slots].reshape(owners * slots)
    codes_far = table_far[:, 0, :slots].reshape(owners * slots)

    group = lax.all_to_all(
        jnp.broadcast_to(cotan[None], (members, tok_dev, width)), "tensor", 0, 0, tiled=True
    ).reshape(tokens_n, width)
    group_far = swap_core(group, owners)

    gate = gate_pre.astype(f32)
    hidden = (gate * jax.nn.sigmoid(gate) * up_pre.astype(f32)).astype(bf16).T
    hidden_far = swap_core(hidden, owners)

    factor = 1.0 / math.sqrt(tokens_n * owners * CORES)
    quarter = owners // 4 * slots
    whole = jax.ShapeDtypeStruct((quarter, side, side), bf16)
    halved = jax.ShapeDtypeStruct((quarter, side // 2, side), bf16)
    smem = pl.BlockSpec(memory_space=pltpu.SMEM)
    vmem = pl.BlockSpec(memory_space=pltpu.VMEM)
    low1, high1, low2, high2, kept = pl.pallas_call(
        functools.partial(grad_kernel, owners, slots, rows_b, factor),
        out_shape=(whole, whole, halved, halved, jax.ShapeDtypeStruct((quarter, side, side), f32)),
        in_specs=[smem, smem, vmem, vmem, vmem, vmem],
        out_specs=(vmem,) * 5,
        scratch_shapes=[
            pltpu.VMEM((hid_dev, 2 * tokens_n), bf16),
            pltpu.VMEM((2 * tokens_n, width), bf16),
            pltpu.VMEM((hid_dev, width), f32),
        ],
        compiler_params=pltpu.CompilerParams(vmem_limit_bytes=44 * 1024 * 1024),
        cost_estimate=pl.CostEstimate(
            flops=4 * hid_dev * width * tokens_n, bytes_accessed=8 * 2**20, transcendentals=0
        ),
        name="grad_blocks",
    )(place, codes, hidden, hidden_far, group, group_far)

    from_high1 = shift_z(low1, -1, owners).astype(f32)
    from_low1 = shift_z(high1, 1, owners).astype(f32)
    from_high2 = shift_z(low2, -2, owners).astype(f32)
    from_low2 = shift_z(high2, 2, owners).astype(f32)
    part = kept + from_high1 + from_low1 + jnp.concatenate([from_high2, from_low2], axis=1)
    part = part.reshape(owners // 4, slots, side, side)

    half = side // 2
    down = jnp.concatenate([part[1], part[6], part[4, :, :half]], axis=1).astype(bf16)
    up = jnp.concatenate([part[7], part[2], part[4, :, half:]], axis=1).astype(bf16)
    down_got = shift_z(down, -4, owners).astype(f32)
    up_got = shift_z(up, 4, owners).astype(f32)
    mine = part[0] + down_got[:, :side] + up_got[:, :side]
    ahead = part[3] + up_got[:, side : 2 * side]
    ahead = jnp.concatenate([ahead[:, :half] + down_got[:, 2 * side :], ahead[:, half:]], axis=1)
    behind = part[5] + down_got[:, side : 2 * side]
    behind = jnp.concatenate([behind[:, :half], behind[:, half:] + up_got[:, 2 * side :]], axis=1)
    ahead, behind = ahead.astype(bf16), behind.astype(bf16)
    gathered, codes_far, _, _ = lax.optimization_barrier((gathered, codes_far, ahead, behind))
    ahead_got = shift_z(ahead, -12, owners).astype(f32)
    behind_got = shift_z(behind, 12, owners).astype(f32)

    dgate, dup = pl.pallas_call(
        functools.partial(token_kernel, owners, slots, rows_b),
        out_shape=(jax.ShapeDtypeStruct(gate_pre.shape, bf16),) * 2,
        in_specs=[smem, smem, smem, vmem, vmem, vmem, vmem],
        out_specs=(vmem,) * 2,
        scratch_shapes=[pltpu.VMEM((hid_dev, width), bf16)],
        compiler_params=pltpu.CompilerParams(vmem_limit_bytes=40 * 1024 * 1024),
        cost_estimate=pl.CostEstimate(
            flops=2 * hid_dev * width * tokens_n, bytes_accessed=16 * 2**20, transcendentals=2**17
        ),
        name="token_grads",
    )(place, codes, codes_far, gathered, group, gate_pre, up_pre)

    mine, dgate, dup = lax.optimization_barrier((mine, dgate, dup))
    tile_grad = mine + ahead_got + behind_got
    return (dgate, dup, tile_grad)


def solution(mesh):
    placed = (
        P(("dp", "tensor"), None),
        P("dp", "tensor"),
        P("dp", "tensor"),
        P(("dp", "tensor"), None, None),
        P(("dp", "tensor")),
    )
    return jax.shard_map(
        local,
        mesh=mesh,
        in_specs=placed,
        out_specs=(P("dp", "tensor"), P("dp", "tensor"), P(("dp", "tensor"), None, None)),
        check_vma=False,
    )
```

time: 544 us -> 227 us (0.42)
  the two profiles are of different devices: /device:TPU:6 before, /device:TPU:99 now
where the time goes in v1:
time: 227 us
  waiting for transfers between devices  92.3 us (41%)
  starting transfers between devices  79.4 us (35%)
  blocking collectives  20.7 us (9%)
  between operations  14.4 us (6%)
  Pallas kernels  13.5 us (6%)
  local copies, waits for them, and re-layouts  5.08 us (2%)
    ppermute x8, waiting for transfers between devices, shift_z(): return lax.ppermute(value, 'dp', pairs)  55 us
    ppermute x8, starting transfers between devices, shift_z(): return lax.ppermute(value, 'dp', pairs)  41.9 us
    all_to_all x1, starting transfers between devices, local(): lax.all_to_all(jnp.broadcast_to(own, (owners, 1, 128)), 'dp', 0, 0, tiled...  27.1 us
    all_gather x1, waiting for transfers between devices, local(): gathered = lax.all_gather(tiles, 'dp', axis=0, tiled=True)  21.4 us
    all_to_all x1, blocking collectives, local(): lax.all_to_all(jnp.broadcast_to(cotan[None], (members, tok_dev, width)),...  20.7 us
    all_to_all x1, waiting for transfers between devices, local(): lax.all_to_all(jnp.broadcast_to(own, (owners, 1, 128)), 'dp', 0, 0, tiled...  15.2 us
    ppermute x3, starting transfers between devices, swap_core(): return lax.ppermute(value, 'dp', pairs)  10.3 us
    pallas_call x1, Pallas kernels, local(): pl.pallas_call(functools.partial(token_kernel, owners, slots, rows_b), ou...  7.99 us
  transfers between devices with their start and end apart: 13, of which 6 were waited for; matrix products, arithmetic and copies ran while one was open for 1% of the time, Pallas kernels for 6%

profile of v1, /device:TPU:99, one launch (start us, length us, event | category | flops | bytes accessed | tf_op | source)
XLA Modules:
  0.0 226.9 jit_solution(16718574231714571466)
XLA Ops:
  7.2 0.0 all-gather.2.cloned.1.call-start
  7.2 0.7 all-gather.2.cloned.1.call-update
  7.9 0.0 copy-start.3
  7.9 0.0 copy-start.1
  7.9 1.0 broadcast_in_dim.5
  8.9 0.0 copy-start.2
  8.9 20.7 %all_to_all.10 = bf16[16,8,4096]{2,1,0:T(8,128)(2,1)S(1)} all-to-all(bf16[16,8,4096]{2,1,0:T(8,128)(2,1)S(1)} %broadcast_in_dim.5), channel_id=1, replica_groups=mesh['dp'=64,'tensor'=16] {'tensor'}, dimensions={0} | all-to-all | bytes 2097152 | tf_op jit(solution)/shard_map/all_to_all | solution.py:130
  29.6 4.4 %collective-permute-start.1 = (bf16[128,4096]{1,0:T(8,128)(2,1)S(1)}, bf16[128,4096]{1,0:T(8,128)(2,1)S(1)}, u32[]{:S(2)}, u32[]{:S(2)}) collective-permute-start(bf16[128,4096]{1,0:T(8,128)(2,1)S(1)} %bitcast.11), channel_id=1, source_target_pairs={{0,16},{16,0},{32,48},{48,32},{64,80},{80,64},{96,112},{112,96},{1... | collective-permute-start | bytes 3145736 | tf_op jit(solution)/shard_map/ppermute | solution.py:101
  34.0 0.0 copy-done.3
  34.0 0.6 broadcast_in_dim.4
  34.6 27.1 %all-to-all-start = ((s32[32,1,128]{2,1,0:T(1,128)}), s32[32,1,128]{2,1,0:T(1,128)S(1)}, u32[]{:S(2)}, u32[]{:S(2)}) async-start(s32[32,1,128]{2,1,0:T(1,128)} %broadcast_in_dim.4), calls=%async_computation | async-start | bytes 32768 | tf_op jit(solution)/shard_map/all_to_all | solution.py:123
  61.7 0.0 copy-done.1
  61.7 0.2 copy.12
  61.9 0.0 copy-done.2
  61.9 0.2 copy.13
  62.1 0.1 fusion.5.hid_a
  62.3 2.5 %collective-permute-start = (bf16[896,128]{1,0:T(8,128)(2,1)S(1)}, bf16[896,128]{1,0:T(8,128)(2,1)S(1)}, u32[]{:S(2)}, u32[]{:S(2)}) collective-permute-start(bf16[896,128]{1,0:T(8,128)(2,1)S(1)} %fusion.5.hid_a), channel_id=1, source_target_pairs={{0,16},{16,0},{32,48},{48,32},{64,80},{80,64},{96,112},{112,96},{1... | collective-permute-start | bytes 688136 | tf_op jit(solution)/shard_map/ppermute | solution.py:101
  64.8 0.1 pad_add_fusion.place
  64.9 15.2 %all-to-all-done = s32[32,1,128]{2,1,0:T(1,128)S(1)} async-done(((s32[32,1,128]{2,1,0:T(1,128)}), s32[32,1,128]{2,1,0:T(1,128)S(1)}, u32[]{:S(2)}, u32[]{:S(2)}) %all-to-all-start) | async-done | bytes 16416 | tf_op jit(solution)/shard_map/all_to_all | solution.py:123
  80.1 0.1 reshape_squeeze.6.codes
  80.2 0.0 collective-permute-done.hid_b
  80.2 0.0 collective-permute-done.1.cot_b
  80.2 5.5 %grad_blocks.1 = (bf16[24,128,128]{2,1,0:T(8,128)(2,1)S(1)}, bf16[24,128,128]{2,1,0:T(8,128)(2,1)S(1)}, bf16[24,64,128]{2,1,0:T(8,128)(2,1)S(1)}, bf16[24,64,128]{2,1,0:T(8,128)(2,1)S(1)}, f32[24,128,128]{2,1,0:T(8,128)S(1)}) custom-call(s32[3]{0:T(128)S(1)} %pad_add_fusion.place, s32[96]{0:T(128)S(1)} %reshape_squeeze.6.codes, ...), custom_call_target="tpu_custom_call" | custom-call | flops 1879048192 | bytes 8388608 | tf_op jit(solution)/shard_map/grad_blocks/pallas_call | solution.py:145
  85.7 2.9 %collective-permute-start.2 = (bf16[24,128,128]{2,1,0:T(8,128)(2,1)S(1)}, bf16[24,128,128]{2,1,0:T(8,128)(2,1)S(1)}, u32[]{:S(2)}, u32[]{:S(2)}) collective-permute-start(bf16[24,128,128]{2,1,0:T(8,128)(2,1)S(1)} %get-tuple-element.28), channel_id=1, source_target_pairs={{0,992},{16,1008},{32,0},{48,16},{64,32},{80,48},{96,64},{112,80},... | collective-permute-start | bytes 2359304 | tf_op jit(solution)/shard_map/ppermute | solution.py:96
  88.6 3.6 %collective-permute-start.3 = (bf16[24,128,128]{2,1,0:T(8,128)(2,1)S(1)}, bf16[24,128,128]{2,1,0:T(8,128)(2,1)S(1)}, u32[]{:S(2)}, u32[]{:S(2)}) collective-permute-start(bf16[24,128,128]{2,1,0:T(8,128)(2,1)S(1)} %get-tuple-element.29), channel_id=1, source_target_pairs={{0,32},{16,48},{32,64},{48,80},{64,96},{80,112},{96,128},{112,144}... | collective-permute-start | bytes 2359304 | tf_op jit(solution)/shard_map/ppermute | solution.py:96
  92.2 3.7 %collective-permute-start.4 = (bf16[24,64,128]{2,1,0:T(8,128)(2,1)S(1)}, bf16[24,64,128]{2,1,0:T(8,128)(2,1)S(1)}, u32[]{:S(2)}, u32[]{:S(2)}) collective-permute-start(bf16[24,64,128]{2,1,0:T(8,128)(2,1)S(1)} %get-tuple-element.30), channel_id=1, source_target_pairs={{0,960},{16,976},{32,992},{48,1008},{64,0},{80,16},{96,32},{112,48... | collective-permute-start | bytes 1179656 | tf_op jit(solution)/shard_map/ppermute | solution.py:96
  95.9 3.7 %collective-permute-start.5 = (bf16[24,64,128]{2,1,0:T(8,128)(2,1)S(1)}, bf16[24,64,128]{2,1,0:T(8,128)(2,1)S(1)}, u32[]{:S(2)}, u32[]{:S(2)}) collective-permute-start(bf16[24,64,128]{2,1,0:T(8,128)(2,1)S(1)} %get-tuple-element.31), channel_id=1, source_target_pairs={{0,64},{16,80},{32,96},{48,112},{64,128},{80,144},{96,160},{112,17... | collective-permute-start | bytes 1179656 | tf_op jit(solution)/shard_map/ppermute | solution.py:96
  99.6 27.6 %collective-permute-done.4 = bf16[24,64,128]{2,1,0:T(8,128)(2,1)S(1)} collective-permute-done((bf16[24,64,128]{2,1,0:T(8,128)(2,1)S(1)}, bf16[24,64,128]{2,1,0:T(8,128)(2,1)S(1)}, u32[]{:S(2)}, u32[]{:S(2)}) %collective-permute-start.4) | collective-permute-done | bytes 393248 | tf_op jit(solution)/shard_map/ppermute | solution.py:96
  127.2 12.4 %collective-permute-done.5 = bf16[24,64,128]{2,1,0:T(8,128)(2,1)S(1)} collective-permute-done((bf16[24,64,128]{2,1,0:T(8,128)(2,1)S(1)}, bf16[24,64,128]{2,1,0:T(8,128)(2,1)S(1)}, u32[]{:S(2)}, u32[]{:S(2)}) %collective-permute-start.5) | collective-permute-done | bytes 393248 | tf_op jit(solution)/shard_map/ppermute | solution.py:96
  139.6 0.0 collective-permute-done.2
  139.6 0.0 collective-permute-done.3
  139.6 0.5 fusion.8
  140.2 1.9 collective-permute-start.7
  142.1 7.3 %collective-permute-start.6 = (bf16[3,320,128]{2,1,0:T(8,128)(2,1)S(1)}, bf16[3,320,128]{2,1,0:T(8,128)(2,1)S(1)}, u32[]{:S(2)}, u32[]{:S(2)}) collective-permute-start(bf16[3,320,128]{2,1,0:T(8,128)(2,1)S(1)} %pad_maximum_fusion), channel_id=1, source_target_pairs={{0,896},{16,912},{32,928},{48,944},{64,960},{80,976},{96,992},{112... | collective-permute-start | bytes 737288 | tf_op jit(solution)/shard_map/ppermute | solution.py:96
  149.4 3.5 %collective-permute-start.8 = (s32[32,1,128]{2,1,0:T(1,128)S(1)}, s32[32,1,128]{2,1,0:T(1,128)S(1)}, u32[]{:S(2)}, u32[]{:S(2)}) collective-permute-start(s32[32,1,128]{2,1,0:T(1,128)S(1)} %all-to-all-done), channel_id=1, source_target_pairs={{0,16},{16,0},{32,48},{48,32},{64,80},{80,64},{96,112},{112,96},{1... | collective-permute-start | bytes 49160 | tf_op jit(solution)/shard_map/ppermute | solution.py:101
  152.9 14.9 %collective-permute-done.7 = bf16[3,320,128]{2,1,0:T(8,128)(2,1)S(1)} collective-permute-done((bf16[3,320,128]{2,1,0:T(8,128)(2,1)S(1)}, bf16[3,320,128]{2,1,0:T(8,128)(2,1)S(1)}, u32[]{:S(2)}, u32[]{:S(2)}) %collective-permute-start.7) | collective-permute-done | bytes 245792 | tf_op jit(solution)/shard_map/ppermute | solution.py:96
  167.8 0.2 collective-permute-done.6
  168.0 0.1 slice_add_fusion
  168.2 5.9 %collective-permute-start.10 = (bf16[3,128,128]{2,1,0:T(8,128)(2,1)S(1)}, bf16[3,128,128]{2,1,0:T(8,128)(2,1)S(1)}, u32[]{:S(2)}, u32[]{:S(2)}) collective-permute-start(bf16[3,128,128]{2,1,0:T(8,128)(2,1)S(1)} %pad_maximum_fusion.3), channel_id=1, source_target_pairs={{0,384},{16,400},{32,416},{48,432},{64,448},{80,464},{96,480},{112... | collective-permute-start | bytes 294920 | tf_op jit(solution)/shard_map/ppermute | solution.py:96
  174.0 12.9 %collective-permute-start.9 = (bf16[3,128,128]{2,1,0:T(8,128)(2,1)S(1)}, bf16[3,128,128]{2,1,0:T(8,128)(2,1)S(1)}, u32[]{:S(2)}, u32[]{:S(2)}) collective-permute-start(bf16[3,128,128]{2,1,0:T(8,128)(2,1)S(1)} %pad_maximum_fusion.2), channel_id=1, source_target_pairs={{0,640},{16,656},{32,672},{48,688},{64,704},{80,720},{96,736},{112... | collective-permute-start | bytes 294920 | tf_op jit(solution)/shard_map/ppermute | solution.py:96
  187.0 0.0 collective-permute-done.8
  187.1 0.1 reshape_squeeze.7.codes_far
  187.2 21.4 %all-gather.2.cloned.1.call-done.tiles = bf16[192,128,128]{2,1,0:T(8,128)(2,1)} async-done(((bf16[3,128,128]{2,1,0:T(8,128)(2,1)}), bf16[192,128,128]{2,1,0:T(8,128)(2,1)}) %all-gather.2.cloned.1.call-update) | async-done | bytes 6291472 | tf_op jit(solution)/shard_map/all_gather | solution.py:119
  208.6 0.0 copy-start
  208.6 2.8 %copy-done = bf16[192,128,128]{2,1,0:T(8,128)(2,1)S(1)} copy-done((bf16[192,128,128]{2,1,0:T(8,128)(2,1)S(1)}, bf16[192,128,128]{2,1,0:T(8,128)(2,1)}, u32[]{:S(2)}) %copy-start) | copy-done | bytes 6291480
  211.4 8.0 %token_grads.1 = (bf16[128,896]{1,0:T(8,128)(2,1)}, bf16[128,896]{1,0:T(8,128)(2,1)}) custom-call(s32[3]{0:T(128)S(1)} %pad_add_fusion.place, s32[96]{0:T(128)S(1)} %reshape_squeeze.6.codes, s32[96]{0:T(128)S(1)} %reshape_squeeze.7.codes_far, bf16[192,128,128]{2,1,0:T(8,128)(2,1)S(1)} %copy-done, bf16[128,4096]{1,0:T(8,128)(2,1)S(1)} %bitcast.13, ...), custom_call_target="tpu_custom_call" | custom-call | flops 939524096 | bytes 16777216 | tf_op jit(solution)/shard_map/token_grads/pallas_call | solution.py:184
  219.4 0.0 collective-permute-done.10
  219.4 0.0 collective-permute-done.9
  219.4 0.7 convert_add_fusion.1
  (14 shorter events, 0.3 us)
Async XLA Ops:
  7.2 201.4 %all-gather.2.cloned.1.call-start = ((), (), s32[]{:S(2)}) async-start(), calls=%async_computation.2 | async-start | bytes 6389760 | tf_op jit(solution)/shard_map/all_gather | solution.py:119
  7.9 26.1 %copy-start.3 = (s32[3]{0:T(128)S(1)}, s32[3]{0:T(128)}, u32[]{:S(2)}) copy-start(s32[3]{0:T(128)} %param.11) | copy-start | bytes 40
  7.9 53.8 %copy-start.1 = (bf16[128,896]{1,0:T(8,128)(2,1)S(1)}, bf16[128,896]{1,0:T(8,128)(2,1)}, u32[]{:S(2)}) copy-start(bf16[128,896]{1,0:T(8,128)(2,1)} %gate_ref.1) | copy-start | bytes 688132
  8.9 53.0 %copy-start.2 = (bf16[128,896]{1,0:T(8,128)(2,1)S(1)}, bf16[128,896]{1,0:T(8,128)(2,1)}, u32[]{:S(2)}) copy-start(bf16[128,896]{1,0:T(8,128)(2,1)} %up_ref.1) | copy-start | bytes 688132
  29.6 50.6 %collective-permute-start.1 = (bf16[128,4096]{1,0:T(8,128)(2,1)S(1)}, bf16[128,4096]{1,0:T(8,128)(2,1)S(1)}, u32[]{:S(2)}, u32[]{:S(2)}) collective-permute-start(bf16[128,4096]{1,0:T(8,128)(2,1)S(1)} %bitcast.11), channel_id=1, source_target_pairs={{0,16},{16,0},{32,48},{48,32},{64,80},{80,64},{96,112},{112,96},{1... | collective-permute-start | bytes 3145736 | tf_op jit(solution)/shard_map/ppermute | solution.py:101
  34.6 45.4 %all-to-all-start = ((s32[32,1,128]{2,1,0:T(1,128)}), s32[32,1,128]{2,1,0:T(1,128)S(1)}, u32[]{:S(2)}, u32[]{:S(2)}) async-start(s32[32,1,128]{2,1,0:T(1,128)} %broadcast_in_dim.4), calls=%async_computation | async-start | bytes 32768 | tf_op jit(solution)/shard_map/all_to_all | solution.py:123
  62.3 17.9 %collective-permute-start = (bf16[896,128]{1,0:T(8,128)(2,1)S(1)}, bf16[896,128]{1,0:T(8,128)(2,1)S(1)}, u32[]{:S(2)}, u32[]{:S(2)}) collective-permute-start(bf16[896,128]{1,0:T(8,128)(2,1)S(1)} %fusion.5.hid_a), channel_id=1, source_target_pairs={{0,16},{16,0},{32,48},{48,32},{64,80},{80,64},{96,112},{112,96},{1... | collective-permute-start | bytes 688136 | tf_op jit(solution)/shard_map/ppermute | solution.py:101
  85.7 53.9 %collective-permute-start.2 = (bf16[24,128,128]{2,1,0:T(8,128)(2,1)S(1)}, bf16[24,128,128]{2,1,0:T(8,128)(2,1)S(1)}, u32[]{:S(2)}, u32[]{:S(2)}) collective-permute-start(bf16[24,128,128]{2,1,0:T(8,128)(2,1)S(1)} %get-tuple-element.28), channel_id=1, source_target_pairs={{0,992},{16,1008},{32,0},{48,16},{64,32},{80,48},{96,64},{112,80},... | collective-permute-start | bytes 2359304 | tf_op jit(solution)/shard_map/ppermute | solution.py:96
  88.6 50.9 %collective-permute-start.3 = (bf16[24,128,128]{2,1,0:T(8,128)(2,1)S(1)}, bf16[24,128,128]{2,1,0:T(8,128)(2,1)S(1)}, u32[]{:S(2)}, u32[]{:S(2)}) collective-permute-start(bf16[24,128,128]{2,1,0:T(8,128)(2,1)S(1)} %get-tuple-element.29), channel_id=1, source_target_pairs={{0,32},{16,48},{32,64},{48,80},{64,96},{80,112},{96,128},{112,144}... | collective-permute-start | bytes 2359304 | tf_op jit(solution)/shard_map/ppermute | solution.py:96
  92.2 35.0 %collective-permute-start.4 = (bf16[24,64,128]{2,1,0:T(8,128)(2,1)S(1)}, bf16[24,64,128]{2,1,0:T(8,128)(2,1)S(1)}, u32[]{:S(2)}, u32[]{:S(2)}) collective-permute-start(bf16[24,64,128]{2,1,0:T(8,128)(2,1)S(1)} %get-tuple-element.30), channel_id=1, source_target_pairs={{0,960},{16,976},{32,992},{48,1008},{64,0},{80,16},{96,32},{112,48... | collective-permute-start | bytes 1179656 | tf_op jit(solution)/shard_map/ppermute | solution.py:96
  95.9 43.6 %collective-permute-start.5 = (bf16[24,64,128]{2,1,0:T(8,128)(2,1)S(1)}, bf16[24,64,128]{2,1,0:T(8,128)(2,1)S(1)}, u32[]{:S(2)}, u32[]{:S(2)}) collective-permute-start(bf16[24,64,128]{2,1,0:T(8,128)(2,1)S(1)} %get-tuple-element.31), channel_id=1, source_target_pairs={{0,64},{16,80},{32,96},{48,112},{64,128},{80,144},{96,160},{112,17... | collective-permute-start | bytes 1179656 | tf_op jit(solution)/shard_map/ppermute | solution.py:96
  140.2 27.6 %collective-permute-start.7 = (bf16[3,320,128]{2,1,0:T(8,128)(2,1)S(1)}, bf16[3,320,128]{2,1,0:T(8,128)(2,1)S(1)}, u32[]{:S(2)}, u32[]{:S(2)}) collective-permute-start(bf16[3,320,128]{2,1,0:T(8,128)(2,1)S(1)} %pad_maximum_fusion.1), channel_id=1, source_target_pairs={{0,128},{16,144},{32,160},{48,176},{64,192},{80,208},{96,224},{112... | collective-permute-start | bytes 737288 | tf_op jit(solution)/shard_map/ppermute | solution.py:96
  142.1 25.8 %collective-permute-start.6 = (bf16[3,320,128]{2,1,0:T(8,128)(2,1)S(1)}, bf16[3,320,128]{2,1,0:T(8,128)(2,1)S(1)}, u32[]{:S(2)}, u32[]{:S(2)}) collective-permute-start(bf16[3,320,128]{2,1,0:T(8,128)(2,1)S(1)} %pad_maximum_fusion), channel_id=1, source_target_pairs={{0,896},{16,912},{32,928},{48,944},{64,960},{80,976},{96,992},{112... | collective-permute-start | bytes 737288 | tf_op jit(solution)/shard_map/ppermute | solution.py:96
  149.4 37.6 %collective-permute-start.8 = (s32[32,1,128]{2,1,0:T(1,128)S(1)}, s32[32,1,128]{2,1,0:T(1,128)S(1)}, u32[]{:S(2)}, u32[]{:S(2)}) collective-permute-start(s32[32,1,128]{2,1,0:T(1,128)S(1)} %all-to-all-done), channel_id=1, source_target_pairs={{0,16},{16,0},{32,48},{48,32},{64,80},{80,64},{96,112},{112,96},{1... | collective-permute-start | bytes 49160 | tf_op jit(solution)/shard_map/ppermute | solution.py:101
  168.2 51.2 %collective-permute-start.10 = (bf16[3,128,128]{2,1,0:T(8,128)(2,1)S(1)}, bf16[3,128,128]{2,1,0:T(8,128)(2,1)S(1)}, u32[]{:S(2)}, u32[]{:S(2)}) collective-permute-start(bf16[3,128,128]{2,1,0:T(8,128)(2,1)S(1)} %pad_maximum_fusion.3), channel_id=1, source_target_pairs={{0,384},{16,400},{32,416},{48,432},{64,448},{80,464},{96,480},{112... | collective-permute-start | bytes 294920 | tf_op jit(solution)/shard_map/ppermute | solution.py:96
  174.0 45.4 %collective-permute-start.9 = (bf16[3,128,128]{2,1,0:T(8,128)(2,1)S(1)}, bf16[3,128,128]{2,1,0:T(8,128)(2,1)S(1)}, u32[]{:S(2)}, u32[]{:S(2)}) collective-permute-start(bf16[3,128,128]{2,1,0:T(8,128)(2,1)S(1)} %pad_maximum_fusion.2), channel_id=1, source_target_pairs={{0,640},{16,656},{32,672},{48,688},{64,704},{80,720},{96,736},{112... | collective-permute-start | bytes 294920 | tf_op jit(solution)/shard_map/ppermute | solution.py:96
  208.6 2.8 %copy-start = (bf16[192,128,128]{2,1,0:T(8,128)(2,1)S(1)}, bf16[192,128,128]{2,1,0:T(8,128)(2,1)}, u32[]{:S(2)}) copy-start(bf16[192,128,128]{2,1,0:T(8,128)(2,1)} %all-gather.2.cloned.1.call-done.tiles) | copy-start | bytes 18874372
Sparse Core Ops, SparseCore 0:
  10.7 197.8 all-gather.1

commit v2 on v1

--- a/solution.py
+++ b/solution.py
@@ -53,15 +53,17 @@
             kept[at] = block(0, k, i, 0, side)
 
 
-def token_kernel(owners, slots, rows_b, place, codes, codes_far, tiles, cot, gate_ref, up_ref,
-                 dgate, dup, dense):
-    side = tiles.shape[1]
+def token_kernel(owners, slots, rows_b, place, codes, codes_far, same, other, other_far, cot, gate_ref,
+                 up_ref, dgate, dup, dense):
+    side = same.shape[1]
+    parity = lax.rem(place[0], 2)
     first = place[1]
     core = place[2]
+    eighth = owners // 4
     dense[...] = jnp.zeros_like(dense)
 
-    def put(code, at):
-        @pl.when(code >= 0)
+    def put(code, held, tiles, at):
+        @pl.when((code >= 0) & held)
         def _():
             column = code // rows_b - first
             row = lax.rem(code, rows_b)
@@ -70,11 +72,17 @@
                 pl.ds(pl.multiple_of(row * side, side), side),
             ] = tiles[at]
 
-    @pl.loop(0, owners)
-    def _(z):
-        for i in range(slots):
-            put(codes[z * slots + i], (z * CORES + core) * slots + i)
-            put(codes_far[z * slots + i], (z * CORES + 1 - core) * slots + i)
+    @pl.loop(0, owners // 2)
+    def _(n):
+        here = n // eighth == core
+        for table, part in ((codes, core), (codes_far, 1 - core)):
+            for i in range(slots):
+                at = (n * CORES + part) * slots + i
+                put(table[(2 * n + parity) * slots + i], True, same, at)
+                code = table[(2 * n + 1 - parity) * slots + i]
+                at = (lax.rem(n, eighth) * CORES + part) * slots + i
+                put(code, here, other, at)
+                put(code, jnp.logical_not(here), other_far, at)
 
     @pl.loop(0, dense.shape[0] // side)
     def _(n):
@@ -116,7 +124,10 @@
     first = lax.axis_index("tensor") * cols_b
     place = jnp.stack([me // CORES, first, core]).astype(jnp.int32)
 
-    gathered = lax.all_gather(tiles, "dp", axis=0, tiled=True)
+    pairs = [
+        [(2 * n + p) * CORES + c for n in range(owners // 2) for c in range(CORES)] for p in range(2)
+    ]
+    same = lax.all_gather(tiles, "dp", axis=0, tiled=True, axis_index_groups=pairs)
 
     own = jnp.zeros((1, 1, 128), jnp.int32).at[0, 0, :slots].set(tile_block)
     rings = [[z * CORES + c for z in range(owners)] for c in range(CORES)]
@@ -169,6 +180,12 @@
     half = side // 2
     down = jnp.concatenate([part[1], part[6], part[4, :, :half]], axis=1).astype(bf16)
     up = jnp.concatenate([part[7], part[2], part[4, :, half:]], axis=1).astype(bf16)
+    same, _, _ = lax.optimization_barrier((same, down, up))
+    few = owners // 4 * slots
+    at = core * 2 * few
+    from_back = shift_z(lax.dynamic_slice_in_dim(same, at, few), 1, owners)
+    from_fore = shift_z(lax.dynamic_slice_in_dim(same, at + few, few), -1, owners)
+    other = jnp.concatenate([from_back, from_fore])
     down_got = shift_z(down, -4, owners).astype(f32)
     up_got = shift_z(up, 4, owners).astype(f32)
     mine = part[0] + down_got[:, :side] + up_got[:, :side]
@@ -177,14 +194,15 @@
     behind = part[5] + down_got[:, side : 2 * side]
     behind = jnp.concatenate([behind[:, :half], behind[:, half:] + up_got[:, 2 * side :]], axis=1)
     ahead, behind = ahead.astype(bf16), behind.astype(bf16)
-    gathered, codes_far, _, _ = lax.optimization_barrier((gathered, codes_far, ahead, behind))
+    other, codes_far, _, _ = lax.optimization_barrier((other, codes_far, ahead, behind))
+    other_far = swap_core(other, owners)
     ahead_got = shift_z(ahead, -12, owners).astype(f32)
     behind_got = shift_z(behind, 12, owners).astype(f32)
 
     dgate, dup = pl.pallas_call(
         functools.partial(token_kernel, owners, slots, rows_b),
         out_shape=(jax.ShapeDtypeStruct(gate_pre.shape, bf16),) * 2,
-        in_specs=[smem, smem, smem, vmem, vmem, vmem, vmem],
+        in_specs=[smem] * 3 + [vmem] * 6,
         out_specs=(vmem,) * 2,
         scratch_shapes=[pltpu.VMEM((hid_dev, width), bf16)],
         compiler_params=pltpu.CompilerParams(vmem_limit_bytes=40 * 1024 * 1024),
@@ -192,7 +210,7 @@
             flops=2 * hid_dev * width * tokens_n, bytes_accessed=16 * 2**20, transcendentals=2**17
         ),
         name="token_grads",
-    )(place, codes, codes_far, gathered, group, gate_pre, up_pre)
+    )(place, codes, codes_far, same, other, other_far, group, gate_pre, up_pre)
 
     mine, dgate, dup = lax.optimization_barrier((mine, dgate, dup))
     tile_grad = mine + ahead_got + behind_got

time: 227 us -> 256 us (1.13)
  the two profiles are of different devices: /device:TPU:99 before, /device:TPU:1 now
where the time goes in v2:
time: 256 us; the launch traced here: 255 us
  waiting for transfers between devices  99.2 us (39%)
  starting transfers between devices  91.8 us (36%)
  blocking collectives  19.3 us (8%)
  Pallas kernels  15.4 us (6%)
  between operations  14.4 us (6%)
  local copies, waits for them, and re-layouts  7.68 us (3%)
  other arithmetic  7.04 us (3%)
    ppermute x10, waiting for transfers between devices, shift_z(): return lax.ppermute(value, 'dp', pairs)  80.1 us
    ppermute x10, starting transfers between devices, shift_z(): return lax.ppermute(value, 'dp', pairs)  46.4 us
    all_to_all x1, starting transfers between devices, local(): lax.all_to_all(jnp.broadcast_to(own, (owners, 1, 128)), 'dp', 0, 0, tiled...  24 us
    ppermute x4, starting transfers between devices, swap_core(): return lax.ppermute(value, 'dp', pairs)  21.3 us
    all_to_all x1, blocking collectives, local(): lax.all_to_all(jnp.broadcast_to(cotan[None], (members, tok_dev, width)),...  19.3 us
    all_to_all x1, waiting for transfers between devices, local(): lax.all_to_all(jnp.broadcast_to(own, (owners, 1, 128)), 'dp', 0, 0, tiled...  18.4 us
    pallas_call x1, Pallas kernels, local(): pl.pallas_call(functools.partial(token_kernel, owners, slots, rows_b), ou...  8.59 us
    pallas_call x1, Pallas kernels, local(): pl.pallas_call(functools.partial(grad_kernel, owners, slots, rows_b, fact...  6.82 us
  transfers between devices with their start and end apart: 16, of which 6 were waited for; matrix products, arithmetic and copies ran while one was open for 4% of the time, Pallas kernels for 6%

profile of v2, /device:TPU:1, one launch (start us, length us, event | category | flops | bytes accessed | tf_op | source)
XLA Modules:
  0.0 254.8 jit_solution(11918598711595681947)
XLA Ops:
  7.2 0.0 all-gather.2.cloned.1.call-start
  7.2 0.7 all-gather.2.cloned.1.call-update
  7.9 0.0 copy-start.6
  7.9 0.0 copy-start.1
  7.9 1.0 broadcast_in_dim.5
  8.9 0.0 copy-start.2
  8.9 19.3 %all_to_all.10 = bf16[16,8,4096]{2,1,0:T(8,128)(2,1)S(1)} all-to-all(bf16[16,8,4096]{2,1,0:T(8,128)(2,1)S(1)} %broadcast_in_dim.5), channel_id=1, replica_groups=mesh['dp'=64,'tensor'=16] {'tensor'}, dimensions={0} | all-to-all | bytes 2097152 | tf_op jit(solution)/shard_map/all_to_all | solution.py:141
  28.2 12.4 %collective-permute-start.1 = (bf16[128,4096]{1,0:T(8,128)(2,1)S(1)}, bf16[128,4096]{1,0:T(8,128)(2,1)S(1)}, u32[]{:S(2)}, u32[]{:S(2)}) collective-permute-start(bf16[128,4096]{1,0:T(8,128)(2,1)S(1)} %bitcast.11), channel_id=1, source_target_pairs={{0,16},{16,0},{32,48},{48,32},{64,80},{80,64},{96,112},{112,96},{1... | collective-permute-start | bytes 3145736 | tf_op jit(solution)/shard_map/ppermute | solution.py:109
  40.6 0.0 copy-done.6
  40.7 0.6 broadcast_in_dim.4
  41.3 24.0 %all-to-all-start = ((s32[32,1,128]{2,1,0:T(1,128)}), s32[32,1,128]{2,1,0:T(1,128)S(1)}, u32[]{:S(2)}, u32[]{:S(2)}) async-start(s32[32,1,128]{2,1,0:T(1,128)} %broadcast_in_dim.4), calls=%async_computation | async-start | bytes 32768 | tf_op jit(solution)/shard_map/all_to_all | solution.py:134
  65.2 0.0 copy-done.1
  65.2 0.2 copy.12
  65.4 0.0 copy-done.2
  65.4 0.2 copy.13
  65.6 0.1 fusion.5.hid_a
  65.8 2.2 collective-permute-start
  68.0 0.1 pad_add_fusion.place
  68.1 18.4 %all-to-all-done = s32[32,1,128]{2,1,0:T(1,128)S(1)} async-done(((s32[32,1,128]{2,1,0:T(1,128)}), s32[32,1,128]{2,1,0:T(1,128)S(1)}, u32[]{:S(2)}, u32[]{:S(2)}) %all-to-all-start) | async-done | bytes 16416 | tf_op jit(solution)/shard_map/all_to_all | solution.py:134
  86.4 0.0 copy-start.5
  86.5 0.1 reshape_squeeze.6.codes
  86.6 0.0 collective-permute-done.hid_b
  86.6 0.4 copy-done.5
  87.0 0.0 collective-permute-done.1.cot_b
  87.0 0.0 copy-start.3
  87.0 1.0 copy-done.3
  88.0 0.0 copy-start.4
  88.0 1.2 copy-done.4
  89.2 6.8 %grad_blocks.1 = (bf16[24,128,128]{2,1,0:T(8,128)(2,1)}, bf16[24,128,128]{2,1,0:T(8,128)(2,1)}, bf16[24,64,128]{2,1,0:T(8,128)(2,1)}, bf16[24,64,128]{2,1,0:T(8,128)(2,1)}, f32[24,128,128]{2,1,0:T(8,128)S(1)}) custom-call(s32[3]{0:T(128)S(1)} %pad_add_fusion.place, s32[96]{0:T(128)S(1)} %reshape_squeeze.6.codes, bf16[896,128]{1,0:T(8,128)(2,1)S(1)} %fusion.5.hid_a, ...), custom_call_target="tpu_custom_call" | custom-call | flops 1879048192 | bytes 8388608 | tf_op jit(solution)/shard_map/grad_blocks/pallas_call | solution.py:156
  96.0 2.1 collective-permute-start.2
  98.2 3.1 %collective-permute-start.3 = (bf16[24,128,128]{2,1,0:T(8,128)(2,1)}, bf16[24,128,128]{2,1,0:T(8,128)(2,1)}, u32[]{:S(2)}, u32[]{:S(2)}) collective-permute-start(bf16[24,128,128]{2,1,0:T(8,128)(2,1)} %get-tuple-element.30), channel_id=1, source_target_pairs={{0,32},{16,48},{32,64},{48,80},{64,96},{80,112},{96,128},{112,144}... | collective-permute-start | bytes 2359304 | tf_op jit(solution)/shard_map/ppermute | solution.py:104
  101.3 2.0 collective-permute-start.4
  103.4 4.1 %collective-permute-start.5 = (bf16[24,64,128]{2,1,0:T(8,128)(2,1)}, bf16[24,64,128]{2,1,0:T(8,128)(2,1)}, u32[]{:S(2)}, u32[]{:S(2)}) collective-permute-start(bf16[24,64,128]{2,1,0:T(8,128)(2,1)} %get-tuple-element.32), channel_id=1, source_target_pairs={{0,64},{16,80},{32,96},{48,112},{64,128},{80,144},{96,160},{112,17... | collective-permute-start | bytes 1179656 | tf_op jit(solution)/shard_map/ppermute | solution.py:104
  107.6 4.3 %collective-permute-start.10 = (s32[32,1,128]{2,1,0:T(1,128)}, s32[32,1,128]{2,1,0:T(1,128)S(1)}, u32[]{:S(2)}, u32[]{:S(2)}) collective-permute-start(s32[32,1,128]{2,1,0:T(1,128)} %copy-done.5), channel_id=1, source_target_pairs={{0,16},{16,0},{32,48},{48,32},{64,80},{80,64},{96,112},{112,96},{1... | collective-permute-start | bytes 49160 | tf_op jit(solution)/shard_map/ppermute | solution.py:109
  111.8 28.4 %collective-permute-done.4 = bf16[24,64,128]{2,1,0:T(8,128)(2,1)} collective-permute-done((bf16[24,64,128]{2,1,0:T(8,128)(2,1)}, bf16[24,64,128]{2,1,0:T(8,128)(2,1)}, u32[]{:S(2)}, u32[]{:S(2)}) %collective-permute-start.4) | collective-permute-done | bytes 393248 | tf_op jit(solution)/shard_map/ppermute | solution.py:104
  140.2 0.0 collective-permute-done.5
  140.3 0.0 collective-permute-done.2
  140.3 0.0 collective-permute-done.3
  140.3 3.2 %fusion.8 = (bf16[24,128,128]{2,1,0:T(8,128)(2,1)S(1)}, f32[24,128,128]{2,1,0:T(8,128)}) fusion(bf16[24,64,128]{2,1,0:T(8,128)(2,1)} %collective-permute-done.5, bf16[24,64,128]{2,1,0:T(8,128)(2,1)} %collective-permute-done.4, bf16[24,128,128]{2,1,0:T(8,128)(2,1)} %collective-permute-done.3, f32[24,128,128]{2,1,0:T(8,128)S(1)} %get-tuple-element.28, ...), kind=kLoop, calls=%fused_computation.32 | loop fusion | flops 3932160 | bytes 6291456 | tf_op jit(solution)/shard_map/convert.20
  143.6 4.5 %collective-permute-start.7 = (bf16[3,320,128]{2,1,0:T(8,128)(2,1)S(1)}, bf16[3,320,128]{2,1,0:T(8,128)(2,1)S(1)}, u32[]{:S(2)}, u32[]{:S(2)}) collective-permute-start(bf16[3,320,128]{2,1,0:T(8,128)(2,1)S(1)} %pad_maximum_fusion.2), channel_id=1, source_target_pairs={{0,128},{16,144},{32,160},{48,176},{64,192},{80,208},{96,224},{112... | collective-permute-start | bytes 737288 | tf_op jit(solution)/shard_map/ppermute | solution.py:104
  148.1 4.7 %collective-permute-start.6 = (bf16[3,320,128]{2,1,0:T(8,128)(2,1)S(1)}, bf16[3,320,128]{2,1,0:T(8,128)(2,1)S(1)}, u32[]{:S(2)}, u32[]{:S(2)}) collective-permute-start(bf16[3,320,128]{2,1,0:T(8,128)(2,1)S(1)} %pad_maximum_fusion.1), channel_id=1, source_target_pairs={{0,896},{16,912},{32,928},{48,944},{64,960},{80,976},{96,992},{112... | collective-permute-start | bytes 737288 | tf_op jit(solution)/shard_map/ppermute | solution.py:104
  152.8 0.0 all-gather.2.cloned.1.call-done.same
  152.8 2.8 %constant_dynamic-slice_fusion.1 = (bf16[24,128,128]{2,1,0:T(8,128)(2,1)}, bf16[24,128,128]{2,1,0:T(8,128)(2,1)}) fusion(bf16[96,128,128]{2,1,0:T(8,128)(2,1)} %all-gather.2.cloned.1.call-done.same, s32[]{:T(128)S(6)} %select_n.19, s32[]{:T(128)S(6)} %select_n.20), kind=kLoop, calls=%fused_computation.31 | loop fusion | bytes 3145736 | tf_op jit(solution)/shard_map/dynamic_slice | solution.py:186
  155.6 4.9 %collective-permute-start.8 = (bf16[24,128,128]{2,1,0:T(8,128)(2,1)}, bf16[24,128,128]{2,1,0:T(8,128)(2,1)}, u32[]{:S(2)}, u32[]{:S(2)}) collective-permute-start(bf16[24,128,128]{2,1,0:T(8,128)(2,1)} %get-tuple-element.43), channel_id=1, source_target_pairs={{0,32},{16,48},{32,64},{48,80},{64,96},{80,112},{96,128},{112,144}... | collective-permute-start | bytes 2359304 | tf_op jit(solution)/shard_map/ppermute | solution.py:104
  160.5 2.1 collective-permute-start.9
  162.6 0.0 collective-permute-done.10
  162.7 0.1 reshape_squeeze.7.codes_far
  162.8 0.0 collective-permute-done.7
  162.8 0.0 collective-permute-done.6
  162.9 1.2 slice_add_fusion
  164.2 0.0 copy-start
  164.2 25.5 %collective-permute-done.8 = bf16[24,128,128]{2,1,0:T(8,128)(2,1)} collective-permute-done((bf16[24,128,128]{2,1,0:T(8,128)(2,1)}, bf16[24,128,128]{2,1,0:T(8,128)(2,1)}, u32[]{:S(2)}, u32[]{:S(2)}) %collective-permute-start.8) | collective-permute-done | bytes 786464 | tf_op jit(solution)/shard_map/ppermute | solution.py:104
  189.7 5.0 %collective-permute-done.9 = bf16[24,128,128]{2,1,0:T(8,128)(2,1)} collective-permute-done((bf16[24,128,128]{2,1,0:T(8,128)(2,1)}, bf16[24,128,128]{2,1,0:T(8,128)(2,1)}, u32[]{:S(2)}, u32[]{:S(2)}) %collective-permute-start.9) | collective-permute-done | bytes 786464 | tf_op jit(solution)/shard_map/ppermute | solution.py:104
  194.7 1.5 pad_maximum_fusion.other
  196.2 2.4 collective-permute-start.11
  198.6 6.5 %collective-permute-start.13 = (bf16[3,128,128]{2,1,0:T(8,128)(2,1)S(1)}, bf16[3,128,128]{2,1,0:T(8,128)(2,1)S(1)}, u32[]{:S(2)}, u32[]{:S(2)}) collective-permute-start(bf16[3,128,128]{2,1,0:T(8,128)(2,1)S(1)} %pad_maximum_fusion.4), channel_id=1, source_target_pairs={{0,384},{16,400},{32,416},{48,432},{64,448},{80,464},{96,480},{112... | collective-permute-start | bytes 294920 | tf_op jit(solution)/shard_map/ppermute | solution.py:104
  205.1 12.3 %collective-permute-start.12 = (bf16[3,128,128]{2,1,0:T(8,128)(2,1)S(1)}, bf16[3,128,128]{2,1,0:T(8,128)(2,1)S(1)}, u32[]{:S(2)}, u32[]{:S(2)}) collective-permute-start(bf16[3,128,128]{2,1,0:T(8,128)(2,1)S(1)} %pad_maximum_fusion.3), channel_id=1, source_target_pairs={{0,640},{16,656},{32,672},{48,688},{64,704},{80,720},{96,736},{112... | collective-permute-start | bytes 294920 | tf_op jit(solution)/shard_map/ppermute | solution.py:104
  217.4 0.0 collective-permute-done.11.other_far
  217.4 0.0 copy-done
  217.4 8.6 %token_grads.1 = (bf16[128,896]{1,0:T(8,128)(2,1)}, bf16[128,896]{1,0:T(8,128)(2,1)}) custom-call(s32[3]{0:T(128)S(1)} %pad_add_fusion.place, s32[96]{0:T(128)S(1)} %reshape_squeeze.6.codes, s32[96]{0:T(128)S(1)} %reshape_squeeze.7.codes_far, bf16[96,128,128]{2,1,0:T(8,128)(2,1)S(1)} %copy-done, bf16[48,128,128]{2,1,0:T(8,128)(2,1)S(1)} %pad_maximum_fusion.other, ...), custom_call_target="tpu_custom_call" | custom-call | flops 939524096 | bytes 16777216 | tf_op jit(solution)/shard_map/token_grads/pallas_call | solution.py:202
  226.0 5.2 %collective-permute-done.13 = bf16[3,128,128]{2,1,0:T(8,128)(2,1)S(1)} collective-permute-done((bf16[3,128,128]{2,1,0:T(8,128)(2,1)S(1)}, bf16[3,128,128]{2,1,0:T(8,128)(2,1)S(1)}, u32[]{:S(2)}, u32[]{:S(2)}) %collective-permute-start.13) | collective-permute-done | bytes 98336 | tf_op jit(solution)/shard_map/ppermute | solution.py:104
  231.2 16.0 %collective-permute-done.12 = bf16[3,128,128]{2,1,0:T(8,128)(2,1)S(1)} collective-permute-done((bf16[3,128,128]{2,1,0:T(8,128)(2,1)S(1)}, bf16[3,128,128]{2,1,0:T(8,128)(2,1)S(1)}, u32[]{:S(2)}, u32[]{:S(2)}) %collective-permute-start.12) | collective-permute-done | bytes 98336 | tf_op jit(solution)/shard_map/ppermute | solution.py:104
  247.2 0.7 convert_add_fusion.1
  (14 shorter events, 0.3 us)
Async XLA Ops:
  7.2 145.7 %all-gather.2.cloned.1.call-start = ((), (), s32[]{:S(2)}) async-start(), calls=%async_computation.2 | async-start | bytes 3244032 | tf_op jit(solution)/shard_map/all_gather | solution.py:130
  7.9 32.7 %copy-start.6 = (s32[3]{0:T(128)S(1)}, s32[3]{0:T(128)}, u32[]{:S(2)}) copy-start(s32[3]{0:T(128)} %param.11) | copy-start | bytes 40
  7.9 57.3 %copy-start.1 = (bf16[128,896]{1,0:T(8,128)(2,1)S(1)}, bf16[128,896]{1,0:T(8,128)(2,1)}, u32[]{:S(2)}) copy-start(bf16[128,896]{1,0:T(8,128)(2,1)} %gate_ref.1) | copy-start | bytes 688132
  8.9 56.5 %copy-start.2 = (bf16[128,896]{1,0:T(8,128)(2,1)S(1)}, bf16[128,896]{1,0:T(8,128)(2,1)}, u32[]{:S(2)}) copy-start(bf16[128,896]{1,0:T(8,128)(2,1)} %up_ref.1) | copy-start | bytes 688132
  28.2 58.9 %collective-permute-start.1 = (bf16[128,4096]{1,0:T(8,128)(2,1)S(1)}, bf16[128,4096]{1,0:T(8,128)(2,1)S(1)}, u32[]{:S(2)}, u32[]{:S(2)}) collective-permute-start(bf16[128,4096]{1,0:T(8,128)(2,1)S(1)} %bitcast.11), channel_id=1, source_target_pairs={{0,16},{16,0},{32,48},{48,32},{64,80},{80,64},{96,112},{112,96},{1... | collective-permute-start | bytes 3145736 | tf_op jit(solution)/shard_map/ppermute | solution.py:109
  41.3 45.2 %all-to-all-start = ((s32[32,1,128]{2,1,0:T(1,128)}), s32[32,1,128]{2,1,0:T(1,128)S(1)}, u32[]{:S(2)}, u32[]{:S(2)}) async-start(s32[32,1,128]{2,1,0:T(1,128)} %broadcast_in_dim.4), calls=%async_computation | async-start | bytes 32768 | tf_op jit(solution)/shard_map/all_to_all | solution.py:134
  65.8 20.8 %collective-permute-start = (bf16[896,128]{1,0:T(8,128)(2,1)S(1)}, bf16[896,128]{1,0:T(8,128)(2,1)S(1)}, u32[]{:S(2)}, u32[]{:S(2)}) collective-permute-start(bf16[896,128]{1,0:T(8,128)(2,1)S(1)} %fusion.5.hid_a), channel_id=1, source_target_pairs={{0,16},{16,0},{32,48},{48,32},{64,80},{80,64},{96,112},{112,96},{1... | collective-permute-start | bytes 688136 | tf_op jit(solution)/shard_map/ppermute | solution.py:109
  86.4 0.6 copy-start.5
  87.0 1.0 copy-start.3
  88.0 1.2 copy-start.4
  96.0 44.2 %collective-permute-start.2 = (bf16[24,128,128]{2,1,0:T(8,128)(2,1)}, bf16[24,128,128]{2,1,0:T(8,128)(2,1)}, u32[]{:S(2)}, u32[]{:S(2)}) collective-permute-start(bf16[24,128,128]{2,1,0:T(8,128)(2,1)} %get-tuple-element.29), channel_id=1, source_target_pairs={{0,992},{16,1008},{32,0},{48,16},{64,32},{80,48},{96,64},{112,80},... | collective-permute-start | bytes 2359304 | tf_op jit(solution)/shard_map/ppermute | solution.py:104
  98.2 42.1 %collective-permute-start.3 = (bf16[24,128,128]{2,1,0:T(8,128)(2,1)}, bf16[24,128,128]{2,1,0:T(8,128)(2,1)}, u32[]{:S(2)}, u32[]{:S(2)}) collective-permute-start(bf16[24,128,128]{2,1,0:T(8,128)(2,1)} %get-tuple-element.30), channel_id=1, source_target_pairs={{0,32},{16,48},{32,64},{48,80},{64,96},{80,112},{96,128},{112,144}... | collective-permute-start | bytes 2359304 | tf_op jit(solution)/shard_map/ppermute | solution.py:104
  101.3 38.9 %collective-permute-start.4 = (bf16[24,64,128]{2,1,0:T(8,128)(2,1)}, bf16[24,64,128]{2,1,0:T(8,128)(2,1)}, u32[]{:S(2)}, u32[]{:S(2)}) collective-permute-start(bf16[24,64,128]{2,1,0:T(8,128)(2,1)} %get-tuple-element.31), channel_id=1, source_target_pairs={{0,960},{16,976},{32,992},{48,1008},{64,0},{80,16},{96,32},{112,48... | collective-permute-start | bytes 1179656 | tf_op jit(solution)/shard_map/ppermute | solution.py:104
  103.4 36.9 %collective-permute-start.5 = (bf16[24,64,128]{2,1,0:T(8,128)(2,1)}, bf16[24,64,128]{2,1,0:T(8,128)(2,1)}, u32[]{:S(2)}, u32[]{:S(2)}) collective-permute-start(bf16[24,64,128]{2,1,0:T(8,128)(2,1)} %get-tuple-element.32), channel_id=1, source_target_pairs={{0,64},{16,80},{32,96},{48,112},{64,128},{80,144},{96,160},{112,17... | collective-permute-start | bytes 1179656 | tf_op jit(solution)/shard_map/ppermute | solution.py:104
  107.6 55.1 %collective-permute-start.10 = (s32[32,1,128]{2,1,0:T(1,128)}, s32[32,1,128]{2,1,0:T(1,128)S(1)}, u32[]{:S(2)}, u32[]{:S(2)}) collective-permute-start(s32[32,1,128]{2,1,0:T(1,128)} %copy-done.5), channel_id=1, source_target_pairs={{0,16},{16,0},{32,48},{48,32},{64,80},{80,64},{96,112},{112,96},{1... | collective-permute-start | bytes 49160 | tf_op jit(solution)/shard_map/ppermute | solution.py:109
  143.6 19.2 %collective-permute-start.7 = (bf16[3,320,128]{2,1,0:T(8,128)(2,1)S(1)}, bf16[3,320,128]{2,1,0:T(8,128)(2,1)S(1)}, u32[]{:S(2)}, u32[]{:S(2)}) collective-permute-start(bf16[3,320,128]{2,1,0:T(8,128)(2,1)S(1)} %pad_maximum_fusion.2), channel_id=1, source_target_pairs={{0,128},{16,144},{32,160},{48,176},{64,192},{80,208},{96,224},{112... | collective-permute-start | bytes 737288 | tf_op jit(solution)/shard_map/ppermute | solution.py:104
  148.1 14.7 %collective-permute-start.6 = (bf16[3,320,128]{2,1,0:T(8,128)(2,1)S(1)}, bf16[3,320,128]{2,1,0:T(8,128)(2,1)S(1)}, u32[]{:S(2)}, u32[]{:S(2)}) collective-permute-start(bf16[3,320,128]{2,1,0:T(8,128)(2,1)S(1)} %pad_maximum_fusion.1), channel_id=1, source_target_pairs={{0,896},{16,912},{32,928},{48,944},{64,960},{80,976},{96,992},{112... | collective-permute-start | bytes 737288 | tf_op jit(solution)/shard_map/ppermute | solution.py:104
  155.6 34.1 %collective-permute-start.8 = (bf16[24,128,128]{2,1,0:T(8,128)(2,1)}, bf16[24,128,128]{2,1,0:T(8,128)(2,1)}, u32[]{:S(2)}, u32[]{:S(2)}) collective-permute-start(bf16[24,128,128]{2,1,0:T(8,128)(2,1)} %get-tuple-element.43), channel_id=1, source_target_pairs={{0,32},{16,48},{32,64},{48,80},{64,96},{80,112},{96,128},{112,144}... | collective-permute-start | bytes 2359304 | tf_op jit(solution)/shard_map/ppermute | solution.py:104
  160.5 34.2 %collective-permute-start.9 = (bf16[24,128,128]{2,1,0:T(8,128)(2,1)}, bf16[24,128,128]{2,1,0:T(8,128)(2,1)}, u32[]{:S(2)}, u32[]{:S(2)}) collective-permute-start(bf16[24,128,128]{2,1,0:T(8,128)(2,1)} %get-tuple-element.44), channel_id=1, source_target_pairs={{0,992},{16,1008},{32,0},{48,16},{64,32},{80,48},{96,64},{112,80},... | collective-permute-start | bytes 2359304 | tf_op jit(solution)/shard_map/ppermute | solution.py:104
  164.2 53.2 %copy-start = (bf16[96,128,128]{2,1,0:T(8,128)(2,1)S(1)}, bf16[96,128,128]{2,1,0:T(8,128)(2,1)}, u32[]{:S(2)}) copy-start(bf16[96,128,128]{2,1,0:T(8,128)(2,1)} %all-gather.2.cloned.1.call-done.same) | copy-start | bytes 9437188
  196.2 21.2 %collective-permute-start.11 = (bf16[48,128,128]{2,1,0:T(8,128)(2,1)S(1)}, bf16[48,128,128]{2,1,0:T(8,128)(2,1)S(1)}, u32[]{:S(2)}, u32[]{:S(2)}) collective-permute-start(bf16[48,128,128]{2,1,0:T(8,128)(2,1)S(1)} %pad_maximum_fusion.other), channel_id=1, source_target_pairs={{0,16},{16,0},{32,48},{48,32},{64,80},{80,64},{96,112},{112,96},{1... | collective-permute-start | bytes 4718600 | tf_op jit(solution)/shard_map/ppermute | solution.py:109
  198.6 32.7 %collective-permute-start.13 = (bf16[3,128,128]{2,1,0:T(8,128)(2,1)S(1)}, bf16[3,128,128]{2,1,0:T(8,128)(2,1)S(1)}, u32[]{:S(2)}, u32[]{:S(2)}) collective-permute-start(bf16[3,128,128]{2,1,0:T(8,128)(2,1)S(1)} %pad_maximum_fusion.4), channel_id=1, source_target_pairs={{0,384},{16,400},{32,416},{48,432},{64,448},{80,464},{96,480},{112... | collective-permute-start | bytes 294920 | tf_op jit(solution)/shard_map/ppermute | solution.py:104
  205.1 42.1 %collective-permute-start.12 = (bf16[3,128,128]{2,1,0:T(8,128)(2,1)S(1)}, bf16[3,128,128]{2,1,0:T(8,128)(2,1)S(1)}, u32[]{:S(2)}, u32[]{:S(2)}) collective-permute-start(bf16[3,128,128]{2,1,0:T(8,128)(2,1)S(1)} %pad_maximum_fusion.3), channel_id=1, source_target_pairs={{0,640},{16,656},{32,672},{48,688},{64,704},{80,720},{96,736},{112... | collective-permute-start | bytes 294920 | tf_op jit(solution)/shard_map/ppermute | solution.py:104
Sparse Core Ops, SparseCore 0:
  10.7 110.1 all-gather.1

commit v3 on v1

--- a/solution.py
+++ b/solution.py
@@ -54,7 +54,7 @@
 
 
 def token_kernel(owners, slots, rows_b, place, codes, codes_far, tiles, cot, gate_ref, up_ref,
-                 dgate, dup, dense):
+                 dgate, dup, dense, arrived):
     side = tiles.shape[1]
     first = place[1]
     core = place[2]
@@ -65,16 +65,20 @@
         def _():
             column = code // rows_b - first
             row = lax.rem(code, rows_b)
-            dense[
+            target = dense.at[
                 pl.ds(pl.multiple_of(column * side, side), side),
                 pl.ds(pl.multiple_of(row * side, side), side),
-            ] = tiles[at]
+            ]
+            pltpu.make_async_copy(tiles.at[at], target, arrived).start()
 
     @pl.loop(0, owners)
     def _(z):
         for i in range(slots):
             put(codes[z * slots + i], (z * CORES + core) * slots + i)
             put(codes_far[z * slots + i], (z * CORES + 1 - core) * slots + i)
+
+    present = dense.at[: dense.shape[0] // 2]
+    pltpu.make_async_copy(present, present, arrived).wait()
 
     @pl.loop(0, dense.shape[0] // side)
     def _(n):
@@ -184,10 +188,10 @@
     dgate, dup = pl.pallas_call(
         functools.partial(token_kernel, owners, slots, rows_b),
         out_shape=(jax.ShapeDtypeStruct(gate_pre.shape, bf16),) * 2,
-        in_specs=[smem, smem, smem, vmem, vmem, vmem, vmem],
+        in_specs=[smem, smem, smem, pl.BlockSpec(memory_space=pltpu.HBM), vmem, vmem, vmem],
         out_specs=(vmem,) * 2,
-        scratch_shapes=[pltpu.VMEM((hid_dev, width), bf16)],
-        compiler_params=pltpu.CompilerParams(vmem_limit_bytes=40 * 1024 * 1024),
+        scratch_shapes=[pltpu.VMEM((hid_dev, width), bf16), pltpu.SemaphoreType.DMA],
+        compiler_params=pltpu.CompilerParams(vmem_limit_bytes=60 * 1024 * 1024),
         cost_estimate=pl.CostEstimate(
             flops=2 * hid_dev * width * tokens_n, bytes_accessed=16 * 2**20, transcendentals=2**17
         ),

time: 227 us -> 225 us (level)
  the two profiles are of different devices: /device:TPU:99 before, /device:TPU:117 now
where the time goes in v3:
time: 225 us; the launch traced here: 224 us
  waiting for transfers between devices  91.5 us (41%)
  starting transfers between devices  80.3 us (36%)
  blocking collectives  19.4 us (9%)
  between operations  14.4 us (6%)
  Pallas kernels  13.9 us (6%)
  local copies, waits for them, and re-layouts  2.85 us (1%)
    ppermute x8, waiting for transfers between devices, shift_z(): return lax.ppermute(value, 'dp', pairs)  54.4 us
    ppermute x8, starting transfers between devices, shift_z(): return lax.ppermute(value, 'dp', pairs)  41.9 us
    all_to_all x1, starting transfers between devices, local(): lax.all_to_all(jnp.broadcast_to(own, (owners, 1, 128)), 'dp', 0, 0, tiled...  27.1 us
    all_gather x1, waiting for transfers between devices, local(): gathered = lax.all_gather(tiles, 'dp', axis=0, tiled=True)  20.2 us
    all_to_all x1, blocking collectives, local(): lax.all_to_all(jnp.broadcast_to(cotan[None], (members, tok_dev, width)),...  19.4 us
    all_to_all x1, waiting for transfers between devices, local(): lax.all_to_all(jnp.broadcast_to(own, (owners, 1, 128)), 'dp', 0, 0, tiled...  16.2 us
    ppermute x3, starting transfers between devices, swap_core(): return lax.ppermute(value, 'dp', pairs)  11.2 us
    pallas_call x1, Pallas kernels, local(): pl.pallas_call(functools.partial(token_kernel, owners, slots, rows_b), ou...  8.42 us
  transfers between devices with their start and end apart: 13, of which 5 were waited for; matrix products, arithmetic and copies ran while one was open for 2% of the time, Pallas kernels for 6%

profile of v3, /device:TPU:117, one launch (start us, length us, event | category | flops | bytes accessed | tf_op | source)
XLA Modules:
  0.0 224.0 jit_solution(10414810750935197636)
XLA Ops:
  7.2 0.0 all-gather.2.cloned.1.call-start
  7.2 0.7 all-gather.2.cloned.1.call-update
  7.9 0.0 copy-start.5
  7.9 0.0 copy-start.3
  7.9 1.0 broadcast_in_dim.5
  8.9 0.0 copy-start.4
  8.9 19.4 %all_to_all.10 = bf16[16,8,4096]{2,1,0:T(8,128)(2,1)S(1)} all-to-all(bf16[16,8,4096]{2,1,0:T(8,128)(2,1)S(1)} %broadcast_in_dim.5), channel_id=1, replica_groups=mesh['dp'=64,'tensor'=16] {'tensor'}, dimensions={0} | all-to-all | bytes 2097152 | tf_op jit(solution)/shard_map/all_to_all | solution.py:134
  28.3 0.0 copy-start
  28.4 3.8 %collective-permute-start.1 = (bf16[128,4096]{1,0:T(8,128)(2,1)S(1)}, bf16[128,4096]{1,0:T(8,128)(2,1)S(1)}, u32[]{:S(2)}, u32[]{:S(2)}) collective-permute-start(bf16[128,4096]{1,0:T(8,128)(2,1)S(1)} %bitcast.11), channel_id=1, source_target_pairs={{0,16},{16,0},{32,48},{48,32},{64,80},{80,64},{96,112},{112,96},{1... | collective-permute-start | bytes 3145736 | tf_op jit(solution)/shard_map/ppermute | solution.py:105
  32.1 0.0 copy-done.5
  32.1 0.6 broadcast_in_dim.4
  32.8 27.1 %all-to-all-start = ((s32[32,1,128]{2,1,0:T(1,128)}), s32[32,1,128]{2,1,0:T(1,128)S(1)}, u32[]{:S(2)}, u32[]{:S(2)}) async-start(s32[32,1,128]{2,1,0:T(1,128)} %broadcast_in_dim.4), calls=%async_computation | async-start | bytes 32768 | tf_op jit(solution)/shard_map/all_to_all | solution.py:127
  59.9 0.0 copy-done.3
  59.9 0.2 copy.12
  60.1 0.0 copy-done.4
  60.1 0.2 copy.13
  60.3 0.1 fusion.5.hid_a
  60.4 2.5 %collective-permute-start = (bf16[896,128]{1,0:T(8,128)(2,1)S(1)}, bf16[896,128]{1,0:T(8,128)(2,1)S(1)}, u32[]{:S(2)}, u32[]{:S(2)}) collective-permute-start(bf16[896,128]{1,0:T(8,128)(2,1)S(1)} %fusion.5.hid_a), channel_id=1, source_target_pairs={{0,16},{16,0},{32,48},{48,32},{64,80},{80,64},{96,112},{112,96},{1... | collective-permute-start | bytes 688136 | tf_op jit(solution)/shard_map/ppermute | solution.py:105
  62.9 0.1 pad_add_fusion.place
  63.0 0.0 copy-start.2
  63.0 16.2 %all-to-all-done = s32[32,1,128]{2,1,0:T(1,128)S(1)} async-done(((s32[32,1,128]{2,1,0:T(1,128)}), s32[32,1,128]{2,1,0:T(1,128)S(1)}, u32[]{:S(2)}, u32[]{:S(2)}) %all-to-all-start) | async-done | bytes 16416 | tf_op jit(solution)/shard_map/all_to_all | solution.py:127
  79.2 0.1 reshape_squeeze.6.codes
  79.3 0.0 copy-start.1
  79.3 0.0 collective-permute-done.hid_b
  79.4 0.0 collective-permute-done.1.cot_b
  79.4 5.5 %grad_blocks.1 = (bf16[24,128,128]{2,1,0:T(8,128)(2,1)S(1)}, bf16[24,128,128]{2,1,0:T(8,128)(2,1)S(1)}, bf16[24,64,128]{2,1,0:T(8,128)(2,1)S(1)}, bf16[24,64,128]{2,1,0:T(8,128)(2,1)S(1)}, f32[24,128,128]{2,1,0:T(8,128)S(1)}) custom-call(s32[3]{0:T(128)S(1)} %pad_add_fusion.place, s32[96]{0:T(128)S(1)} %reshape_squeeze.6.codes, ...), custom_call_target="tpu_custom_call" | custom-call | flops 1879048192 | bytes 8388608 | tf_op jit(solution)/shard_map/grad_blocks/pallas_call | solution.py:149
  84.8 0.0 copy-done
  84.9 0.0 copy-done.2
  84.9 0.0 copy-done.1
  84.9 1.9 collective-permute-start.2
  86.8 4.6 %collective-permute-start.3 = (bf16[24,128,128]{2,1,0:T(8,128)(2,1)S(1)}, bf16[24,128,128]{2,1,0:T(8,128)(2,1)S(1)}, u32[]{:S(2)}, u32[]{:S(2)}) collective-permute-start(bf16[24,128,128]{2,1,0:T(8,128)(2,1)S(1)} %get-tuple-element.29), channel_id=1, source_target_pairs={{0,32},{16,48},{32,64},{48,80},{64,96},{80,112},{96,128},{112,144}... | collective-permute-start | bytes 2359304 | tf_op jit(solution)/shard_map/ppermute | solution.py:100
  91.4 1.9 collective-permute-start.4
  93.3 5.5 %collective-permute-start.5 = (bf16[24,64,128]{2,1,0:T(8,128)(2,1)S(1)}, bf16[24,64,128]{2,1,0:T(8,128)(2,1)S(1)}, u32[]{:S(2)}, u32[]{:S(2)}) collective-permute-start(bf16[24,64,128]{2,1,0:T(8,128)(2,1)S(1)} %get-tuple-element.31), channel_id=1, source_target_pairs={{0,64},{16,80},{32,96},{48,112},{64,128},{80,144},{96,160},{112,17... | collective-permute-start | bytes 1179656 | tf_op jit(solution)/shard_map/ppermute | solution.py:100
  98.8 23.2 %collective-permute-done.4 = bf16[24,64,128]{2,1,0:T(8,128)(2,1)S(1)} collective-permute-done((bf16[24,64,128]{2,1,0:T(8,128)(2,1)S(1)}, bf16[24,64,128]{2,1,0:T(8,128)(2,1)S(1)}, u32[]{:S(2)}, u32[]{:S(2)}) %collective-permute-start.4) | collective-permute-done | bytes 393248 | tf_op jit(solution)/shard_map/ppermute | solution.py:100
  122.0 13.2 %collective-permute-done.5 = bf16[24,64,128]{2,1,0:T(8,128)(2,1)S(1)} collective-permute-done((bf16[24,64,128]{2,1,0:T(8,128)(2,1)S(1)}, bf16[24,64,128]{2,1,0:T(8,128)(2,1)S(1)}, u32[]{:S(2)}, u32[]{:S(2)}) %collective-permute-start.5) | collective-permute-done | bytes 393248 | tf_op jit(solution)/shard_map/ppermute | solution.py:100
  135.2 0.0 collective-permute-done.2
  135.2 0.0 collective-permute-done.3
  135.2 0.5 fusion.8
  135.8 4.0 %collective-permute-start.7 = (bf16[3,320,128]{2,1,0:T(8,128)(2,1)S(1)}, bf16[3,320,128]{2,1,0:T(8,128)(2,1)S(1)}, u32[]{:S(2)}, u32[]{:S(2)}) collective-permute-start(bf16[3,320,128]{2,1,0:T(8,128)(2,1)S(1)} %pad_maximum_fusion.1), channel_id=1, source_target_pairs={{0,128},{16,144},{32,160},{48,176},{64,192},{80,208},{96,224},{112... | collective-permute-start | bytes 737288 | tf_op jit(solution)/shard_map/ppermute | solution.py:100
  139.9 5.2 %collective-permute-start.6 = (bf16[3,320,128]{2,1,0:T(8,128)(2,1)S(1)}, bf16[3,320,128]{2,1,0:T(8,128)(2,1)S(1)}, u32[]{:S(2)}, u32[]{:S(2)}) collective-permute-start(bf16[3,320,128]{2,1,0:T(8,128)(2,1)S(1)} %pad_maximum_fusion), channel_id=1, source_target_pairs={{0,896},{16,912},{32,928},{48,944},{64,960},{80,976},{96,992},{112... | collective-permute-start | bytes 737288 | tf_op jit(solution)/shard_map/ppermute | solution.py:100
  145.0 5.0 %collective-permute-start.8 = (s32[32,1,128]{2,1,0:T(1,128)S(1)}, s32[32,1,128]{2,1,0:T(1,128)S(1)}, u32[]{:S(2)}, u32[]{:S(2)}) collective-permute-start(s32[32,1,128]{2,1,0:T(1,128)S(1)} %all-to-all-done), channel_id=1, source_target_pairs={{0,16},{16,0},{32,48},{48,32},{64,80},{80,64},{96,112},{112,96},{1... | collective-permute-start | bytes 49160 | tf_op jit(solution)/shard_map/ppermute | solution.py:105
  150.0 18.0 %collective-permute-done.7 = bf16[3,320,128]{2,1,0:T(8,128)(2,1)S(1)} collective-permute-done((bf16[3,320,128]{2,1,0:T(8,128)(2,1)S(1)}, bf16[3,320,128]{2,1,0:T(8,128)(2,1)S(1)}, u32[]{:S(2)}, u32[]{:S(2)}) %collective-permute-start.7) | collective-permute-done | bytes 245792 | tf_op jit(solution)/shard_map/ppermute | solution.py:100
  168.0 0.0 collective-permute-done.6
  168.1 0.1 slice_add_fusion
  168.2 4.7 %collective-permute-start.10 = (bf16[3,128,128]{2,1,0:T(8,128)(2,1)S(1)}, bf16[3,128,128]{2,1,0:T(8,128)(2,1)S(1)}, u32[]{:S(2)}, u32[]{:S(2)}) collective-permute-start(bf16[3,128,128]{2,1,0:T(8,128)(2,1)S(1)} %pad_maximum_fusion.3), channel_id=1, source_target_pairs={{0,384},{16,400},{32,416},{48,432},{64,448},{80,464},{96,480},{112... | collective-permute-start | bytes 294920 | tf_op jit(solution)/shard_map/ppermute | solution.py:100
  172.9 14.1 %collective-permute-start.9 = (bf16[3,128,128]{2,1,0:T(8,128)(2,1)S(1)}, bf16[3,128,128]{2,1,0:T(8,128)(2,1)S(1)}, u32[]{:S(2)}, u32[]{:S(2)}) collective-permute-start(bf16[3,128,128]{2,1,0:T(8,128)(2,1)S(1)} %pad_maximum_fusion.2), channel_id=1, source_target_pairs={{0,640},{16,656},{32,672},{48,688},{64,704},{80,720},{96,736},{112... | collective-permute-start | bytes 294920 | tf_op jit(solution)/shard_map/ppermute | solution.py:100
  187.1 0.0 collective-permute-done.8
  187.1 0.6 reshape_squeeze.7.codes_far
  187.8 20.2 %all-gather.2.cloned.1.call-done.tiles = bf16[192,128,128]{2,1,0:T(8,128)(2,1)} async-done(((bf16[3,128,128]{2,1,0:T(8,128)(2,1)}), bf16[192,128,128]{2,1,0:T(8,128)(2,1)}) %all-gather.2.cloned.1.call-update) | async-done | bytes 6291472 | tf_op jit(solution)/shard_map/all_gather | solution.py:123
  208.0 8.4 %token_grads.1 = (bf16[128,896]{1,0:T(8,128)(2,1)}, bf16[128,896]{1,0:T(8,128)(2,1)}) custom-call(s32[3]{0:T(128)} %copy-done.2, s32[96]{0:T(128)} %copy-done.1, s32[96]{0:T(128)} %reshape_squeeze.7.codes_far, bf16[192,128,128]{2,1,0:T(8,128)(2,1)} %all-gather.2.cloned.1.call-done.tiles, bf16[128,4096]{1,0:T(8,128)(2,1)} %bitcast.13, ...), custom_call_target="tpu_custom_call" | custom-call | flops 939524096 | bytes 16777216 | tf_op jit(solution)/shard_map/token_grads/pallas_call | solution.py:188
  216.4 0.0 collective-permute-done.10
  216.4 0.0 collective-permute-done.9
  216.4 0.7 convert_add_fusion.1
  (14 shorter events, 0.3 us)
Async XLA Ops:
  7.2 200.8 %all-gather.2.cloned.1.call-start = ((), (), s32[]{:S(2)}) async-start(), calls=%async_computation.2 | async-start | bytes 6389760 | tf_op jit(solution)/shard_map/all_gather | solution.py:123
  7.9 24.2 %copy-start.5 = (s32[3]{0:T(128)S(1)}, s32[3]{0:T(128)}, u32[]{:S(2)}) copy-start(s32[3]{0:T(128)} %param.11) | copy-start | bytes 40
  7.9 52.0 %copy-start.3 = (bf16[128,896]{1,0:T(8,128)(2,1)S(1)}, bf16[128,896]{1,0:T(8,128)(2,1)}, u32[]{:S(2)}) copy-start(bf16[128,896]{1,0:T(8,128)(2,1)} %gate_ref.1) | copy-start | bytes 688132
  8.9 51.2 %copy-start.4 = (bf16[128,896]{1,0:T(8,128)(2,1)S(1)}, bf16[128,896]{1,0:T(8,128)(2,1)}, u32[]{:S(2)}) copy-start(bf16[128,896]{1,0:T(8,128)(2,1)} %up_ref.1) | copy-start | bytes 688132
  28.3 56.5 %copy-start = (bf16[16,8,4096]{2,1,0:T(8,128)(2,1)}, bf16[16,8,4096]{2,1,0:T(8,128)(2,1)S(1)}, u32[]{:S(2)}) copy-start(bf16[16,8,4096]{2,1,0:T(8,128)(2,1)S(1)} %all_to_all.10) | copy-start | bytes 3145732
  28.4 51.0 %collective-permute-start.1 = (bf16[128,4096]{1,0:T(8,128)(2,1)S(1)}, bf16[128,4096]{1,0:T(8,128)(2,1)S(1)}, u32[]{:S(2)}, u32[]{:S(2)}) collective-permute-start(bf16[128,4096]{1,0:T(8,128)(2,1)S(1)} %bitcast.11), channel_id=1, source_target_pairs={{0,16},{16,0},{32,48},{48,32},{64,80},{80,64},{96,112},{112,96},{1... | collective-permute-start | bytes 3145736 | tf_op jit(solution)/shard_map/ppermute | solution.py:105
  32.8 46.4 %all-to-all-start = ((s32[32,1,128]{2,1,0:T(1,128)}), s32[32,1,128]{2,1,0:T(1,128)S(1)}, u32[]{:S(2)}, u32[]{:S(2)}) async-start(s32[32,1,128]{2,1,0:T(1,128)} %broadcast_in_dim.4), calls=%async_computation | async-start | bytes 32768 | tf_op jit(solution)/shard_map/all_to_all | solution.py:127
  60.4 18.9 %collective-permute-start = (bf16[896,128]{1,0:T(8,128)(2,1)S(1)}, bf16[896,128]{1,0:T(8,128)(2,1)S(1)}, u32[]{:S(2)}, u32[]{:S(2)}) collective-permute-start(bf16[896,128]{1,0:T(8,128)(2,1)S(1)} %fusion.5.hid_a), channel_id=1, source_target_pairs={{0,16},{16,0},{32,48},{48,32},{64,80},{80,64},{96,112},{112,96},{1... | collective-permute-start | bytes 688136 | tf_op jit(solution)/shard_map/ppermute | solution.py:105
  63.0 21.8 %copy-start.2 = (s32[3]{0:T(128)}, s32[3]{0:T(128)S(1)}, u32[]{:S(2)}) copy-start(s32[3]{0:T(128)S(1)} %pad_add_fusion.place) | copy-start | bytes 40
  79.3 5.5 %copy-start.1 = (s32[96]{0:T(128)}, s32[96]{0:T(128)S(1)}, u32[]{:S(2)}) copy-start(s32[96]{0:T(128)S(1)} %reshape_squeeze.6.codes) | copy-start | bytes 1156
  84.9 50.3 %collective-permute-start.2 = (bf16[24,128,128]{2,1,0:T(8,128)(2,1)S(1)}, bf16[24,128,128]{2,1,0:T(8,128)(2,1)S(1)}, u32[]{:S(2)}, u32[]{:S(2)}) collective-permute-start(bf16[24,128,128]{2,1,0:T(8,128)(2,1)S(1)} %get-tuple-element.28), channel_id=1, source_target_pairs={{0,992},{16,1008},{32,0},{48,16},{64,32},{80,48},{96,64},{112,80},... | collective-permute-start | bytes 2359304 | tf_op jit(solution)/shard_map/ppermute | solution.py:100
  86.8 48.4 %collective-permute-start.3 = (bf16[24,128,128]{2,1,0:T(8,128)(2,1)S(1)}, bf16[24,128,128]{2,1,0:T(8,128)(2,1)S(1)}, u32[]{:S(2)}, u32[]{:S(2)}) collective-permute-start(bf16[24,128,128]{2,1,0:T(8,128)(2,1)S(1)} %get-tuple-element.29), channel_id=1, source_target_pairs={{0,32},{16,48},{32,64},{48,80},{64,96},{80,112},{96,128},{112,144}... | collective-permute-start | bytes 2359304 | tf_op jit(solution)/shard_map/ppermute | solution.py:100
  91.4 30.6 %collective-permute-start.4 = (bf16[24,64,128]{2,1,0:T(8,128)(2,1)S(1)}, bf16[24,64,128]{2,1,0:T(8,128)(2,1)S(1)}, u32[]{:S(2)}, u32[]{:S(2)}) collective-permute-start(bf16[24,64,128]{2,1,0:T(8,128)(2,1)S(1)} %get-tuple-element.30), channel_id=1, source_target_pairs={{0,960},{16,976},{32,992},{48,1008},{64,0},{80,16},{96,32},{112,48... | collective-permute-start | bytes 1179656 | tf_op jit(solution)/shard_map/ppermute | solution.py:100
  93.3 41.9 %collective-permute-start.5 = (bf16[24,64,128]{2,1,0:T(8,128)(2,1)S(1)}, bf16[24,64,128]{2,1,0:T(8,128)(2,1)S(1)}, u32[]{:S(2)}, u32[]{:S(2)}) collective-permute-start(bf16[24,64,128]{2,1,0:T(8,128)(2,1)S(1)} %get-tuple-element.31), channel_id=1, source_target_pairs={{0,64},{16,80},{32,96},{48,112},{64,128},{80,144},{96,160},{112,17... | collective-permute-start | bytes 1179656 | tf_op jit(solution)/shard_map/ppermute | solution.py:100
  135.8 32.2 %collective-permute-start.7 = (bf16[3,320,128]{2,1,0:T(8,128)(2,1)S(1)}, bf16[3,320,128]{2,1,0:T(8,128)(2,1)S(1)}, u32[]{:S(2)}, u32[]{:S(2)}) collective-permute-start(bf16[3,320,128]{2,1,0:T(8,128)(2,1)S(1)} %pad_maximum_fusion.1), channel_id=1, source_target_pairs={{0,128},{16,144},{32,160},{48,176},{64,192},{80,208},{96,224},{112... | collective-permute-start | bytes 737288 | tf_op jit(solution)/shard_map/ppermute | solution.py:100
  139.9 28.1 %collective-permute-start.6 = (bf16[3,320,128]{2,1,0:T(8,128)(2,1)S(1)}, bf16[3,320,128]{2,1,0:T(8,128)(2,1)S(1)}, u32[]{:S(2)}, u32[]{:S(2)}) collective-permute-start(bf16[3,320,128]{2,1,0:T(8,128)(2,1)S(1)} %pad_maximum_fusion), channel_id=1, source_target_pairs={{0,896},{16,912},{32,928},{48,944},{64,960},{80,976},{96,992},{112... | collective-permute-start | bytes 737288 | tf_op jit(solution)/shard_map/ppermute | solution.py:100
  145.0 42.1 %collective-permute-start.8 = (s32[32,1,128]{2,1,0:T(1,128)S(1)}, s32[32,1,128]{2,1,0:T(1,128)S(1)}, u32[]{:S(2)}, u32[]{:S(2)}) collective-permute-start(s32[32,1,128]{2,1,0:T(1,128)S(1)} %all-to-all-done), channel_id=1, source_target_pairs={{0,16},{16,0},{32,48},{48,32},{64,80},{80,64},{96,112},{112,96},{1... | collective-permute-start | bytes 49160 | tf_op jit(solution)/shard_map/ppermute | solution.py:105
  168.2 48.2 %collective-permute-start.10 = (bf16[3,128,128]{2,1,0:T(8,128)(2,1)S(1)}, bf16[3,128,128]{2,1,0:T(8,128)(2,1)S(1)}, u32[]{:S(2)}, u32[]{:S(2)}) collective-permute-start(bf16[3,128,128]{2,1,0:T(8,128)(2,1)S(1)} %pad_maximum_fusion.3), channel_id=1, source_target_pairs={{0,384},{16,400},{32,416},{48,432},{64,448},{80,464},{96,480},{112... | collective-permute-start | bytes 294920 | tf_op jit(solution)/shard_map/ppermute | solution.py:100
  172.9 43.5 %collective-permute-start.9 = (bf16[3,128,128]{2,1,0:T(8,128)(2,1)S(1)}, bf16[3,128,128]{2,1,0:T(8,128)(2,1)S(1)}, u32[]{:S(2)}, u32[]{:S(2)}) collective-permute-start(bf16[3,128,128]{2,1,0:T(8,128)(2,1)S(1)} %pad_maximum_fusion.2), channel_id=1, source_target_pairs={{0,640},{16,656},{32,672},{48,688},{64,704},{80,720},{96,736},{112... | collective-permute-start | bytes 294920 | tf_op jit(solution)/shard_map/ppermute | solution.py:100
Sparse Core Ops, SparseCore 0:
  10.7 197.2 all-gather.1

commit v4 on v3

--- a/solution.py
+++ b/solution.py
@@ -58,6 +58,8 @@
     side = tiles.shape[1]
     first = place[1]
     core = place[2]
+    columns = dense.shape[0] // side
+    split = (columns + 1) // 2
     dense[...] = jnp.zeros_like(dense)
 
     def put(code, at):
@@ -69,7 +71,7 @@
                 pl.ds(pl.multiple_of(column * side, side), side),
                 pl.ds(pl.multiple_of(row * side, side), side),
             ]
-            pltpu.make_async_copy(tiles.at[at], target, arrived).start()
+            pltpu.make_async_copy(tiles.at[at], target, arrived.at[column // split]).start()
 
     @pl.loop(0, owners)
     def _(z):
@@ -77,12 +79,10 @@
             put(codes[z * slots + i], (z * CORES + core) * slots + i)
             put(codes_far[z * slots + i], (z * CORES + 1 - core) * slots + i)
 
-    present = dense.at[: dense.shape[0] // 2]
-    pltpu.make_async_copy(present, present, arrived).wait()
-
-    @pl.loop(0, dense.shape[0] // side)
-    def _(n):
-        cols = pl.ds(pl.multiple_of(n * side, side), side)
+    for part, (low, high) in enumerate(((0, split), (split, columns))):
+        present = dense.at[: (high - low) * side // 2]
+        pltpu.make_async_copy(present, present, arrived.at[part]).wait()
+        cols = slice(low * side, high * side)
         dhid = lax.dot_general(
             cot[...], dense[cols, :], (((1,), (1,)), ((), ())), preferred_element_type=jnp.float32
         )
@@ -190,7 +190,7 @@
         out_shape=(jax.ShapeDtypeStruct(gate_pre.shape, bf16),) * 2,
         in_specs=[smem, smem, smem, pl.BlockSpec(memory_space=pltpu.HBM), vmem, vmem, vmem],
         out_specs=(vmem,) * 2,
-        scratch_shapes=[pltpu.VMEM((hid_dev, width), bf16), pltpu.SemaphoreType.DMA],
+        scratch_shapes=[pltpu.VMEM((hid_dev, width), bf16), pltpu.SemaphoreType.DMA((2,))],
         compiler_params=pltpu.CompilerParams(vmem_limit_bytes=60 * 1024 * 1024),
         cost_estimate=pl.CostEstimate(
             flops=2 * hid_dev * width * tokens_n, bytes_accessed=16 * 2**20, transcendentals=2**17

time: 225 us -> 225 us (level)
  no operation moved by 1% of the time
where the time goes in v4:
time: 225 us
  waiting for transfers between devices  91.5 us (41%)
  starting transfers between devices  80.3 us (36%)
  blocking collectives  19.4 us (9%)
  Pallas kernels  14.6 us (6%)
  between operations  14.4 us (6%)
  local copies, waits for them, and re-layouts  2.85 us (1%)
    ppermute x8, waiting for transfers between devices, shift_z(): return lax.ppermute(value, 'dp', pairs)  54.4 us
    ppermute x8, starting transfers between devices, shift_z(): return lax.ppermute(value, 'dp', pairs)  41.9 us
    all_to_all x1, starting transfers between devices, local(): lax.all_to_all(jnp.broadcast_to(own, (owners, 1, 128)), 'dp', 0, 0, tiled...  27.1 us
    all_gather x1, waiting for transfers between devices, local(): gathered = lax.all_gather(tiles, 'dp', axis=0, tiled=True)  20.2 us
    all_to_all x1, blocking collectives, local(): lax.all_to_all(jnp.broadcast_to(cotan[None], (members, tok_dev, width)),...  19.4 us
    all_to_all x1, waiting for transfers between devices, local(): lax.all_to_all(jnp.broadcast_to(own, (owners, 1, 128)), 'dp', 0, 0, tiled...  16.2 us
    ppermute x3, starting transfers between devices, swap_core(): return lax.ppermute(value, 'dp', pairs)  11.2 us
    pallas_call x1, Pallas kernels, local(): pl.pallas_call(functools.partial(token_kernel, owners, slots, rows_b), ou...  9.1 us
  transfers between devices with their start and end apart: 13, of which 5 were waited for; matrix products, arithmetic and copies ran while one was open for 2% of the time, Pallas kernels for 6%

profile of v4, /device:TPU:117, one launch (start us, length us, event | category | flops | bytes accessed | tf_op | source)
XLA Modules:
  0.0 224.7 jit_solution(8907484583936172977)
XLA Ops:
  7.2 0.0 all-gather.2.cloned.1.call-start
  7.2 0.7 all-gather.2.cloned.1.call-update
  7.9 0.0 copy-start.5
  7.9 0.0 copy-start.3
  7.9 1.0 broadcast_in_dim.5
  8.9 0.0 copy-start.4
  8.9 19.4 %all_to_all.10 = bf16[16,8,4096]{2,1,0:T(8,128)(2,1)S(1)} all-to-all(bf16[16,8,4096]{2,1,0:T(8,128)(2,1)S(1)} %broadcast_in_dim.5), channel_id=1, replica_groups=mesh['dp'=64,'tensor'=16] {'tensor'}, dimensions={0} | all-to-all | bytes 2097152 | tf_op jit(solution)/shard_map/all_to_all | solution.py:134
  28.3 0.0 copy-start
  28.4 3.8 %collective-permute-start.1 = (bf16[128,4096]{1,0:T(8,128)(2,1)S(1)}, bf16[128,4096]{1,0:T(8,128)(2,1)S(1)}, u32[]{:S(2)}, u32[]{:S(2)}) collective-permute-start(bf16[128,4096]{1,0:T(8,128)(2,1)S(1)} %bitcast.11), channel_id=1, source_target_pairs={{0,16},{16,0},{32,48},{48,32},{64,80},{80,64},{96,112},{112,96},{1... | collective-permute-start | bytes 3145736 | tf_op jit(solution)/shard_map/ppermute | solution.py:105
  32.1 0.0 copy-done.5
  32.1 0.6 broadcast_in_dim.4
  32.8 27.1 %all-to-all-start = ((s32[32,1,128]{2,1,0:T(1,128)}), s32[32,1,128]{2,1,0:T(1,128)S(1)}, u32[]{:S(2)}, u32[]{:S(2)}) async-start(s32[32,1,128]{2,1,0:T(1,128)} %broadcast_in_dim.4), calls=%async_computation | async-start | bytes 32768 | tf_op jit(solution)/shard_map/all_to_all | solution.py:127
  59.9 0.0 copy-done.3
  59.9 0.2 copy.12
  60.1 0.0 copy-done.4
  60.1 0.2 copy.13
  60.3 0.1 fusion.5.hid_a
  60.4 2.5 %collective-permute-start = (bf16[896,128]{1,0:T(8,128)(2,1)S(1)}, bf16[896,128]{1,0:T(8,128)(2,1)S(1)}, u32[]{:S(2)}, u32[]{:S(2)}) collective-permute-start(bf16[896,128]{1,0:T(8,128)(2,1)S(1)} %fusion.5.hid_a), channel_id=1, source_target_pairs={{0,16},{16,0},{32,48},{48,32},{64,80},{80,64},{96,112},{112,96},{1... | collective-permute-start | bytes 688136 | tf_op jit(solution)/shard_map/ppermute | solution.py:105
  62.9 0.1 pad_add_fusion.place
  63.0 0.0 copy-start.2
  63.0 16.2 %all-to-all-done = s32[32,1,128]{2,1,0:T(1,128)S(1)} async-done(((s32[32,1,128]{2,1,0:T(1,128)}), s32[32,1,128]{2,1,0:T(1,128)S(1)}, u32[]{:S(2)}, u32[]{:S(2)}) %all-to-all-start) | async-done | bytes 16416 | tf_op jit(solution)/shard_map/all_to_all | solution.py:127
  79.2 0.1 reshape_squeeze.6.codes
  79.3 0.0 copy-start.1
  79.3 0.0 collective-permute-done.hid_b
  79.4 0.0 collective-permute-done.1.cot_b
  79.4 5.5 %grad_blocks.1 = (bf16[24,128,128]{2,1,0:T(8,128)(2,1)S(1)}, bf16[24,128,128]{2,1,0:T(8,128)(2,1)S(1)}, bf16[24,64,128]{2,1,0:T(8,128)(2,1)S(1)}, bf16[24,64,128]{2,1,0:T(8,128)(2,1)S(1)}, f32[24,128,128]{2,1,0:T(8,128)S(1)}) custom-call(s32[3]{0:T(128)S(1)} %pad_add_fusion.place, s32[96]{0:T(128)S(1)} %reshape_squeeze.6.codes, ...), custom_call_target="tpu_custom_call" | custom-call | flops 1879048192 | bytes 8388608 | tf_op jit(solution)/shard_map/grad_blocks/pallas_call | solution.py:149
  84.8 0.0 copy-done
  84.9 0.0 copy-done.2
  84.9 0.0 copy-done.1
  84.9 1.9 collective-permute-start.2
  86.8 4.6 %collective-permute-start.3 = (bf16[24,128,128]{2,1,0:T(8,128)(2,1)S(1)}, bf16[24,128,128]{2,1,0:T(8,128)(2,1)S(1)}, u32[]{:S(2)}, u32[]{:S(2)}) collective-permute-start(bf16[24,128,128]{2,1,0:T(8,128)(2,1)S(1)} %get-tuple-element.29), channel_id=1, source_target_pairs={{0,32},{16,48},{32,64},{48,80},{64,96},{80,112},{96,128},{112,144}... | collective-permute-start | bytes 2359304 | tf_op jit(solution)/shard_map/ppermute | solution.py:100
  91.4 1.9 collective-permute-start.4
  93.3 5.5 %collective-permute-start.5 = (bf16[24,64,128]{2,1,0:T(8,128)(2,1)S(1)}, bf16[24,64,128]{2,1,0:T(8,128)(2,1)S(1)}, u32[]{:S(2)}, u32[]{:S(2)}) collective-permute-start(bf16[24,64,128]{2,1,0:T(8,128)(2,1)S(1)} %get-tuple-element.31), channel_id=1, source_target_pairs={{0,64},{16,80},{32,96},{48,112},{64,128},{80,144},{96,160},{112,17... | collective-permute-start | bytes 1179656 | tf_op jit(solution)/shard_map/ppermute | solution.py:100
  98.8 23.2 %collective-permute-done.4 = bf16[24,64,128]{2,1,0:T(8,128)(2,1)S(1)} collective-permute-done((bf16[24,64,128]{2,1,0:T(8,128)(2,1)S(1)}, bf16[24,64,128]{2,1,0:T(8,128)(2,1)S(1)}, u32[]{:S(2)}, u32[]{:S(2)}) %collective-permute-start.4) | collective-permute-done | bytes 393248 | tf_op jit(solution)/shard_map/ppermute | solution.py:100
  122.0 13.2 %collective-permute-done.5 = bf16[24,64,128]{2,1,0:T(8,128)(2,1)S(1)} collective-permute-done((bf16[24,64,128]{2,1,0:T(8,128)(2,1)S(1)}, bf16[24,64,128]{2,1,0:T(8,128)(2,1)S(1)}, u32[]{:S(2)}, u32[]{:S(2)}) %collective-permute-start.5) | collective-permute-done | bytes 393248 | tf_op jit(solution)/shard_map/ppermute | solution.py:100
  135.2 0.0 collective-permute-done.2
  135.2 0.0 collective-permute-done.3
  135.2 0.5 fusion.8
  135.8 4.0 %collective-permute-start.7 = (bf16[3,320,128]{2,1,0:T(8,128)(2,1)S(1)}, bf16[3,320,128]{2,1,0:T(8,128)(2,1)S(1)}, u32[]{:S(2)}, u32[]{:S(2)}) collective-permute-start(bf16[3,320,128]{2,1,0:T(8,128)(2,1)S(1)} %pad_maximum_fusion.1), channel_id=1, source_target_pairs={{0,128},{16,144},{32,160},{48,176},{64,192},{80,208},{96,224},{112... | collective-permute-start | bytes 737288 | tf_op jit(solution)/shard_map/ppermute | solution.py:100
  139.9 5.2 %collective-permute-start.6 = (bf16[3,320,128]{2,1,0:T(8,128)(2,1)S(1)}, bf16[3,320,128]{2,1,0:T(8,128)(2,1)S(1)}, u32[]{:S(2)}, u32[]{:S(2)}) collective-permute-start(bf16[3,320,128]{2,1,0:T(8,128)(2,1)S(1)} %pad_maximum_fusion), channel_id=1, source_target_pairs={{0,896},{16,912},{32,928},{48,944},{64,960},{80,976},{96,992},{112... | collective-permute-start | bytes 737288 | tf_op jit(solution)/shard_map/ppermute | solution.py:100
  145.0 5.0 %collective-permute-start.8 = (s32[32,1,128]{2,1,0:T(1,128)S(1)}, s32[32,1,128]{2,1,0:T(1,128)S(1)}, u32[]{:S(2)}, u32[]{:S(2)}) collective-permute-start(s32[32,1,128]{2,1,0:T(1,128)S(1)} %all-to-all-done), channel_id=1, source_target_pairs={{0,16},{16,0},{32,48},{48,32},{64,80},{80,64},{96,112},{112,96},{1... | collective-permute-start | bytes 49160 | tf_op jit(solution)/shard_map/ppermute | solution.py:105
  150.0 18.0 %collective-permute-done.7 = bf16[3,320,128]{2,1,0:T(8,128)(2,1)S(1)} collective-permute-done((bf16[3,320,128]{2,1,0:T(8,128)(2,1)S(1)}, bf16[3,320,128]{2,1,0:T(8,128)(2,1)S(1)}, u32[]{:S(2)}, u32[]{:S(2)}) %collective-permute-start.7) | collective-permute-done | bytes 245792 | tf_op jit(solution)/shard_map/ppermute | solution.py:100
  168.0 0.0 collective-permute-done.6
  168.1 0.1 slice_add_fusion
  168.2 4.7 %collective-permute-start.10 = (bf16[3,128,128]{2,1,0:T(8,128)(2,1)S(1)}, bf16[3,128,128]{2,1,0:T(8,128)(2,1)S(1)}, u32[]{:S(2)}, u32[]{:S(2)}) collective-permute-start(bf16[3,128,128]{2,1,0:T(8,128)(2,1)S(1)} %pad_maximum_fusion.3), channel_id=1, source_target_pairs={{0,384},{16,400},{32,416},{48,432},{64,448},{80,464},{96,480},{112... | collective-permute-start | bytes 294920 | tf_op jit(solution)/shard_map/ppermute | solution.py:100
  172.9 14.1 %collective-permute-start.9 = (bf16[3,128,128]{2,1,0:T(8,128)(2,1)S(1)}, bf16[3,128,128]{2,1,0:T(8,128)(2,1)S(1)}, u32[]{:S(2)}, u32[]{:S(2)}) collective-permute-start(bf16[3,128,128]{2,1,0:T(8,128)(2,1)S(1)} %pad_maximum_fusion.2), channel_id=1, source_target_pairs={{0,640},{16,656},{32,672},{48,688},{64,704},{80,720},{96,736},{112... | collective-permute-start | bytes 294920 | tf_op jit(solution)/shard_map/ppermute | solution.py:100
  187.1 0.0 collective-permute-done.8
  187.1 0.6 reshape_squeeze.7.codes_far
  187.8 20.2 %all-gather.2.cloned.1.call-done.tiles = bf16[192,128,128]{2,1,0:T(8,128)(2,1)} async-done(((bf16[3,128,128]{2,1,0:T(8,128)(2,1)}), bf16[192,128,128]{2,1,0:T(8,128)(2,1)}) %all-gather.2.cloned.1.call-update) | async-done | bytes 6291472 | tf_op jit(solution)/shard_map/all_gather | solution.py:123
  208.0 9.1 %token_grads.1 = (bf16[128,896]{1,0:T(8,128)(2,1)}, bf16[128,896]{1,0:T(8,128)(2,1)}) custom-call(s32[3]{0:T(128)} %copy-done.2, s32[96]{0:T(128)} %copy-done.1, s32[96]{0:T(128)} %reshape_squeeze.7.codes_far, bf16[192,128,128]{2,1,0:T(8,128)(2,1)} %all-gather.2.cloned.1.call-done.tiles, bf16[128,4096]{1,0:T(8,128)(2,1)} %bitcast.13, ...), custom_call_target="tpu_custom_call" | custom-call | flops 939524096 | bytes 16777216 | tf_op jit(solution)/shard_map/token_grads/pallas_call | solution.py:188
  217.1 0.0 collective-permute-done.10
  217.1 0.0 collective-permute-done.9
  217.1 0.7 convert_add_fusion.1
  (14 shorter events, 0.3 us)
Async XLA Ops:
  7.2 200.8 %all-gather.2.cloned.1.call-start = ((), (), s32[]{:S(2)}) async-start(), calls=%async_computation.2 | async-start | bytes 6389760 | tf_op jit(solution)/shard_map/all_gather | solution.py:123
  7.9 24.2 %copy-start.5 = (s32[3]{0:T(128)S(1)}, s32[3]{0:T(128)}, u32[]{:S(2)}) copy-start(s32[3]{0:T(128)} %param.11) | copy-start | bytes 40
  7.9 52.0 %copy-start.3 = (bf16[128,896]{1,0:T(8,128)(2,1)S(1)}, bf16[128,896]{1,0:T(8,128)(2,1)}, u32[]{:S(2)}) copy-start(bf16[128,896]{1,0:T(8,128)(2,1)} %gate_ref.1) | copy-start | bytes 688132
  8.9 51.2 %copy-start.4 = (bf16[128,896]{1,0:T(8,128)(2,1)S(1)}, bf16[128,896]{1,0:T(8,128)(2,1)}, u32[]{:S(2)}) copy-start(bf16[128,896]{1,0:T(8,128)(2,1)} %up_ref.1) | copy-start | bytes 688132
  28.3 56.5 %copy-start = (bf16[16,8,4096]{2,1,0:T(8,128)(2,1)}, bf16[16,8,4096]{2,1,0:T(8,128)(2,1)S(1)}, u32[]{:S(2)}) copy-start(bf16[16,8,4096]{2,1,0:T(8,128)(2,1)S(1)} %all_to_all.10) | copy-start | bytes 3145732
  28.4 51.0 %collective-permute-start.1 = (bf16[128,4096]{1,0:T(8,128)(2,1)S(1)}, bf16[128,4096]{1,0:T(8,128)(2,1)S(1)}, u32[]{:S(2)}, u32[]{:S(2)}) collective-permute-start(bf16[128,4096]{1,0:T(8,128)(2,1)S(1)} %bitcast.11), channel_id=1, source_target_pairs={{0,16},{16,0},{32,48},{48,32},{64,80},{80,64},{96,112},{112,96},{1... | collective-permute-start | bytes 3145736 | tf_op jit(solution)/shard_map/ppermute | solution.py:105
  32.8 46.4 %all-to-all-start = ((s32[32,1,128]{2,1,0:T(1,128)}), s32[32,1,128]{2,1,0:T(1,128)S(1)}, u32[]{:S(2)}, u32[]{:S(2)}) async-start(s32[32,1,128]{2,1,0:T(1,128)} %broadcast_in_dim.4), calls=%async_computation | async-start | bytes 32768 | tf_op jit(solution)/shard_map/all_to_all | solution.py:127
  60.4 18.9 %collective-permute-start = (bf16[896,128]{1,0:T(8,128)(2,1)S(1)}, bf16[896,128]{1,0:T(8,128)(2,1)S(1)}, u32[]{:S(2)}, u32[]{:S(2)}) collective-permute-start(bf16[896,128]{1,0:T(8,128)(2,1)S(1)} %fusion.5.hid_a), channel_id=1, source_target_pairs={{0,16},{16,0},{32,48},{48,32},{64,80},{80,64},{96,112},{112,96},{1... | collective-permute-start | bytes 688136 | tf_op jit(solution)/shard_map/ppermute | solution.py:105
  63.0 21.8 %copy-start.2 = (s32[3]{0:T(128)}, s32[3]{0:T(128)S(1)}, u32[]{:S(2)}) copy-start(s32[3]{0:T(128)S(1)} %pad_add_fusion.place) | copy-start | bytes 40
  79.3 5.5 %copy-start.1 = (s32[96]{0:T(128)}, s32[96]{0:T(128)S(1)}, u32[]{:S(2)}) copy-start(s32[96]{0:T(128)S(1)} %reshape_squeeze.6.codes) | copy-start | bytes 1156
  84.9 50.3 %collective-permute-start.2 = (bf16[24,128,128]{2,1,0:T(8,128)(2,1)S(1)}, bf16[24,128,128]{2,1,0:T(8,128)(2,1)S(1)}, u32[]{:S(2)}, u32[]{:S(2)}) collective-permute-start(bf16[24,128,128]{2,1,0:T(8,128)(2,1)S(1)} %get-tuple-element.28), channel_id=1, source_target_pairs={{0,992},{16,1008},{32,0},{48,16},{64,32},{80,48},{96,64},{112,80},... | collective-permute-start | bytes 2359304 | tf_op jit(solution)/shard_map/ppermute | solution.py:100
  86.8 48.4 %collective-permute-start.3 = (bf16[24,128,128]{2,1,0:T(8,128)(2,1)S(1)}, bf16[24,128,128]{2,1,0:T(8,128)(2,1)S(1)}, u32[]{:S(2)}, u32[]{:S(2)}) collective-permute-start(bf16[24,128,128]{2,1,0:T(8,128)(2,1)S(1)} %get-tuple-element.29), channel_id=1, source_target_pairs={{0,32},{16,48},{32,64},{48,80},{64,96},{80,112},{96,128},{112,144}... | collective-permute-start | bytes 2359304 | tf_op jit(solution)/shard_map/ppermute | solution.py:100
  91.4 30.6 %collective-permute-start.4 = (bf16[24,64,128]{2,1,0:T(8,128)(2,1)S(1)}, bf16[24,64,128]{2,1,0:T(8,128)(2,1)S(1)}, u32[]{:S(2)}, u32[]{:S(2)}) collective-permute-start(bf16[24,64,128]{2,1,0:T(8,128)(2,1)S(1)} %get-tuple-element.30), channel_id=1, source_target_pairs={{0,960},{16,976},{32,992},{48,1008},{64,0},{80,16},{96,32},{112,48... | collective-permute-start | bytes 1179656 | tf_op jit(solution)/shard_map/ppermute | solution.py:100
  93.3 41.9 %collective-permute-start.5 = (bf16[24,64,128]{2,1,0:T(8,128)(2,1)S(1)}, bf16[24,64,128]{2,1,0:T(8,128)(2,1)S(1)}, u32[]{:S(2)}, u32[]{:S(2)}) collective-permute-start(bf16[24,64,128]{2,1,0:T(8,128)(2,1)S(1)} %get-tuple-element.31), channel_id=1, source_target_pairs={{0,64},{16,80},{32,96},{48,112},{64,128},{80,144},{96,160},{112,17... | collective-permute-start | bytes 1179656 | tf_op jit(solution)/shard_map/ppermute | solution.py:100
  135.8 32.2 %collective-permute-start.7 = (bf16[3,320,128]{2,1,0:T(8,128)(2,1)S(1)}, bf16[3,320,128]{2,1,0:T(8,128)(2,1)S(1)}, u32[]{:S(2)}, u32[]{:S(2)}) collective-permute-start(bf16[3,320,128]{2,1,0:T(8,128)(2,1)S(1)} %pad_maximum_fusion.1), channel_id=1, source_target_pairs={{0,128},{16,144},{32,160},{48,176},{64,192},{80,208},{96,224},{112... | collective-permute-start | bytes 737288 | tf_op jit(solution)/shard_map/ppermute | solution.py:100
  139.9 28.1 %collective-permute-start.6 = (bf16[3,320,128]{2,1,0:T(8,128)(2,1)S(1)}, bf16[3,320,128]{2,1,0:T(8,128)(2,1)S(1)}, u32[]{:S(2)}, u32[]{:S(2)}) collective-permute-start(bf16[3,320,128]{2,1,0:T(8,128)(2,1)S(1)} %pad_maximum_fusion), channel_id=1, source_target_pairs={{0,896},{16,912},{32,928},{48,944},{64,960},{80,976},{96,992},{112... | collective-permute-start | bytes 737288 | tf_op jit(solution)/shard_map/ppermute | solution.py:100
  145.0 42.1 %collective-permute-start.8 = (s32[32,1,128]{2,1,0:T(1,128)S(1)}, s32[32,1,128]{2,1,0:T(1,128)S(1)}, u32[]{:S(2)}, u32[]{:S(2)}) collective-permute-start(s32[32,1,128]{2,1,0:T(1,128)S(1)} %all-to-all-done), channel_id=1, source_target_pairs={{0,16},{16,0},{32,48},{48,32},{64,80},{80,64},{96,112},{112,96},{1... | collective-permute-start | bytes 49160 | tf_op jit(solution)/shard_map/ppermute | solution.py:105
  168.2 48.9 %collective-permute-start.10 = (bf16[3,128,128]{2,1,0:T(8,128)(2,1)S(1)}, bf16[3,128,128]{2,1,0:T(8,128)(2,1)S(1)}, u32[]{:S(2)}, u32[]{:S(2)}) collective-permute-start(bf16[3,128,128]{2,1,0:T(8,128)(2,1)S(1)} %pad_maximum_fusion.3), channel_id=1, source_target_pairs={{0,384},{16,400},{32,416},{48,432},{64,448},{80,464},{96,480},{112... | collective-permute-start | bytes 294920 | tf_op jit(solution)/shard_map/ppermute | solution.py:100
  172.9 44.2 %collective-permute-start.9 = (bf16[3,128,128]{2,1,0:T(8,128)(2,1)S(1)}, bf16[3,128,128]{2,1,0:T(8,128)(2,1)S(1)}, u32[]{:S(2)}, u32[]{:S(2)}) collective-permute-start(bf16[3,128,128]{2,1,0:T(8,128)(2,1)S(1)} %pad_maximum_fusion.2), channel_id=1, source_target_pairs={{0,640},{16,656},{32,672},{48,688},{64,704},{80,720},{96,736},{112... | collective-permute-start | bytes 294920 | tf_op jit(solution)/shard_map/ppermute | solution.py:100
Sparse Core Ops, SparseCore 0:
  10.7 197.2 all-gather.1

commit v5 on v3

--- a/solution.py
+++ b/solution.py
@@ -56,22 +56,21 @@
 def token_kernel(owners, slots, rows_b, place, codes, codes_far, tiles, cot, gate_ref, up_ref,
                  dgate, dup, dense, arrived):
     side = tiles.shape[1]
-    first = place[1]
     core = place[2]
     dense[...] = jnp.zeros_like(dense)
 
     def put(code, at):
         @pl.when(code >= 0)
         def _():
-            column = code // rows_b - first
-            row = lax.rem(code, rows_b)
+            column = lax.div(code, rows_b)
+            row = code - column * rows_b
             target = dense.at[
                 pl.ds(pl.multiple_of(column * side, side), side),
                 pl.ds(pl.multiple_of(row * side, side), side),
             ]
             pltpu.make_async_copy(tiles.at[at], target, arrived).start()
 
-    @pl.loop(0, owners)
+    @pl.loop(0, owners, unroll=4)
     def _(z):
         for i in range(slots):
             put(codes[z * slots + i], (z * CORES + core) * slots + i)
@@ -181,7 +180,11 @@
     behind = part[5] + down_got[:, side : 2 * side]
     behind = jnp.concatenate([behind[:, :half], behind[:, half:] + up_got[:, 2 * side :]], axis=1)
     ahead, behind = ahead.astype(bf16), behind.astype(bf16)
-    gathered, codes_far, _, _ = lax.optimization_barrier((gathered, codes_far, ahead, behind))
+    def inside(table):
+        return jnp.where(table >= 0, table - first * rows_b, -1)
+
+    near, far = inside(codes), inside(codes_far)
+    gathered, near, far, _, _ = lax.optimization_barrier((gathered, near, far, ahead, behind))
     ahead_got = shift_z(ahead, -12, owners).astype(f32)
     behind_got = shift_z(behind, 12, owners).astype(f32)
 
@@ -196,7 +199,7 @@
             flops=2 * hid_dev * width * tokens_n, bytes_accessed=16 * 2**20, transcendentals=2**17
         ),
         name="token_grads",
-    )(place, codes, codes_far, gathered, group, gate_pre, up_pre)
+    )(place, near, far, gathered, group, gate_pre, up_pre)
 
     mine, dgate, dup = lax.optimization_barrier((mine, dgate, dup))
     tile_grad = mine + ahead_got + behind_got

time: 225 us -> 225 us (level)
  the two profiles are of different devices: /device:TPU:117 before, /device:TPU:111 now
where the time goes in v5:
time: 225 us; the launch traced here: 224 us
  waiting for transfers between devices  90.9 us (40%)
  starting transfers between devices  79.9 us (36%)
  blocking collectives  20.1 us (9%)
  between operations  14.4 us (6%)
  Pallas kernels  13.5 us (6%)
  local copies, waits for them, and re-layouts  2.86 us (1%)
  other arithmetic  2.25 us (1%)
    ppermute x8, waiting for transfers between devices, shift_z(): return lax.ppermute(value, 'dp', pairs)  55.2 us
    ppermute x8, starting transfers between devices, shift_z(): return lax.ppermute(value, 'dp', pairs)  41.9 us
    all_to_all x1, starting transfers between devices, local(): lax.all_to_all(jnp.broadcast_to(own, (owners, 1, 128)), 'dp', 0, 0, tiled...  27.1 us
    all_to_all x1, blocking collectives, local(): lax.all_to_all(jnp.broadcast_to(cotan[None], (members, tok_dev, width)),...  20.1 us
    all_gather x1, waiting for transfers between devices, local(): gathered = lax.all_gather(tiles, 'dp', axis=0, tiled=True)  20 us
    all_to_all x1, waiting for transfers between devices, local(): lax.all_to_all(jnp.broadcast_to(own, (owners, 1, 128)), 'dp', 0, 0, tiled...  15.1 us
    ppermute x3, starting transfers between devices, swap_core(): return lax.ppermute(value, 'dp', pairs)  10.9 us
    pallas_call x1, Pallas kernels, local(): pl.pallas_call(functools.partial(token_kernel, owners, slots, rows_b), ou...  7.98 us
  transfers between devices with their start and end apart: 13, of which 5 were waited for; matrix products, arithmetic and copies ran while one was open for 2% of the time, Pallas kernels for 6%

profile of v5, /device:TPU:111, one launch (start us, length us, event | category | flops | bytes accessed | tf_op | source)
XLA Modules:
  0.0 223.9 jit_solution(10815915271343774057)
XLA Ops:
  7.2 0.0 all-gather.2.cloned.1.call-start
  7.2 0.7 all-gather.2.cloned.1.call-update
  7.9 0.0 copy-start.4
  7.9 0.0 copy-start.2
  7.9 1.0 broadcast_in_dim.20
  8.9 0.0 copy-start.3
  8.9 20.1 %all_to_all.10 = bf16[16,8,4096]{2,1,0:T(8,128)(2,1)S(1)} all-to-all(bf16[16,8,4096]{2,1,0:T(8,128)(2,1)S(1)} %broadcast_in_dim.20), channel_id=1, replica_groups=mesh['dp'=64,'tensor'=16] {'tensor'}, dimensions={0} | all-to-all | bytes 2097152 | tf_op jit(solution)/shard_map/all_to_all | solution.py:133
  29.0 0.0 copy-start
  29.0 4.0 %collective-permute-start.1 = (bf16[128,4096]{1,0:T(8,128)(2,1)S(1)}, bf16[128,4096]{1,0:T(8,128)(2,1)S(1)}, u32[]{:S(2)}, u32[]{:S(2)}) collective-permute-start(bf16[128,4096]{1,0:T(8,128)(2,1)S(1)} %bitcast.11), channel_id=1, source_target_pairs={{0,16},{16,0},{32,48},{48,32},{64,80},{80,64},{96,112},{112,96},{1... | collective-permute-start | bytes 3145736 | tf_op jit(solution)/shard_map/ppermute | solution.py:104
  33.0 0.0 copy-done.4
  33.0 0.6 broadcast_in_dim.19
  33.6 27.1 %all-to-all-start = ((s32[32,1,128]{2,1,0:T(1,128)}), s32[32,1,128]{2,1,0:T(1,128)S(1)}, u32[]{:S(2)}, u32[]{:S(2)}) async-start(s32[32,1,128]{2,1,0:T(1,128)} %broadcast_in_dim.19), calls=%async_computation | async-start | bytes 32768 | tf_op jit(solution)/shard_map/all_to_all | solution.py:126
  60.8 0.0 copy-done.2
  60.8 0.2 copy.12
  61.0 0.0 copy-done.3
  61.0 0.2 copy.13
  61.2 0.1 fusion.5.hid_a
  61.3 2.5 %collective-permute-start = (bf16[896,128]{1,0:T(8,128)(2,1)S(1)}, bf16[896,128]{1,0:T(8,128)(2,1)S(1)}, u32[]{:S(2)}, u32[]{:S(2)}) collective-permute-start(bf16[896,128]{1,0:T(8,128)(2,1)S(1)} %fusion.5.hid_a), channel_id=1, source_target_pairs={{0,16},{16,0},{32,48},{48,32},{64,80},{80,64},{96,112},{112,96},{1... | collective-permute-start | bytes 688136 | tf_op jit(solution)/shard_map/ppermute | solution.py:104
  63.8 0.1 pad_add_fusion.place
  63.9 0.0 copy-start.1
  63.9 15.1 %all-to-all-done = s32[32,1,128]{2,1,0:T(1,128)S(1)} async-done(((s32[32,1,128]{2,1,0:T(1,128)}), s32[32,1,128]{2,1,0:T(1,128)S(1)}, u32[]{:S(2)}, u32[]{:S(2)}) %all-to-all-start) | async-done | bytes 16416 | tf_op jit(solution)/shard_map/all_to_all | solution.py:126
  79.1 0.1 reshape_squeeze.4.codes
  79.2 0.0 collective-permute-done.hid_b
  79.2 0.0 collective-permute-done.1.cot_b
  79.2 5.5 %grad_blocks.1 = (bf16[24,128,128]{2,1,0:T(8,128)(2,1)S(1)}, bf16[24,128,128]{2,1,0:T(8,128)(2,1)S(1)}, bf16[24,64,128]{2,1,0:T(8,128)(2,1)S(1)}, bf16[24,64,128]{2,1,0:T(8,128)(2,1)S(1)}, f32[24,128,128]{2,1,0:T(8,128)S(1)}) custom-call(s32[3]{0:T(128)S(1)} %pad_add_fusion.place, s32[96]{0:T(128)S(1)} %reshape_squeeze.4.codes, ...), custom_call_target="tpu_custom_call" | custom-call | flops 1879048192 | bytes 8388608 | tf_op jit(solution)/shard_map/grad_blocks/pallas_call | solution.py:148
  84.7 0.0 copy-done
  84.7 0.0 copy-done.1
  84.7 2.9 %collective-permute-start.2 = (bf16[24,128,128]{2,1,0:T(8,128)(2,1)S(1)}, bf16[24,128,128]{2,1,0:T(8,128)(2,1)S(1)}, u32[]{:S(2)}, u32[]{:S(2)}) collective-permute-start(bf16[24,128,128]{2,1,0:T(8,128)(2,1)S(1)} %get-tuple-element.29), channel_id=1, source_target_pairs={{0,992},{16,1008},{32,0},{48,16},{64,32},{80,48},{96,64},{112,80},... | collective-permute-start | bytes 2359304 | tf_op jit(solution)/shard_map/ppermute | solution.py:99
  87.6 3.6 %collective-permute-start.3 = (bf16[24,128,128]{2,1,0:T(8,128)(2,1)S(1)}, bf16[24,128,128]{2,1,0:T(8,128)(2,1)S(1)}, u32[]{:S(2)}, u32[]{:S(2)}) collective-permute-start(bf16[24,128,128]{2,1,0:T(8,128)(2,1)S(1)} %get-tuple-element.30), channel_id=1, source_target_pairs={{0,32},{16,48},{32,64},{48,80},{64,96},{80,112},{96,128},{112,144}... | collective-permute-start | bytes 2359304 | tf_op jit(solution)/shard_map/ppermute | solution.py:99
  91.2 3.6 %collective-permute-start.4 = (bf16[24,64,128]{2,1,0:T(8,128)(2,1)S(1)}, bf16[24,64,128]{2,1,0:T(8,128)(2,1)S(1)}, u32[]{:S(2)}, u32[]{:S(2)}) collective-permute-start(bf16[24,64,128]{2,1,0:T(8,128)(2,1)S(1)} %get-tuple-element.31), channel_id=1, source_target_pairs={{0,960},{16,976},{32,992},{48,1008},{64,0},{80,16},{96,32},{112,48... | collective-permute-start | bytes 1179656 | tf_op jit(solution)/shard_map/ppermute | solution.py:99
  94.8 3.8 %collective-permute-start.5 = (bf16[24,64,128]{2,1,0:T(8,128)(2,1)S(1)}, bf16[24,64,128]{2,1,0:T(8,128)(2,1)S(1)}, u32[]{:S(2)}, u32[]{:S(2)}) collective-permute-start(bf16[24,64,128]{2,1,0:T(8,128)(2,1)S(1)} %get-tuple-element.32), channel_id=1, source_target_pairs={{0,64},{16,80},{32,96},{48,112},{64,128},{80,144},{96,160},{112,17... | collective-permute-start | bytes 1179656 | tf_op jit(solution)/shard_map/ppermute | solution.py:99
  98.6 25.4 %collective-permute-done.4 = bf16[24,64,128]{2,1,0:T(8,128)(2,1)S(1)} collective-permute-done((bf16[24,64,128]{2,1,0:T(8,128)(2,1)S(1)}, bf16[24,64,128]{2,1,0:T(8,128)(2,1)S(1)}, u32[]{:S(2)}, u32[]{:S(2)}) %collective-permute-start.4) | collective-permute-done | bytes 393248 | tf_op jit(solution)/shard_map/ppermute | solution.py:99
  124.1 13.5 %collective-permute-done.5 = bf16[24,64,128]{2,1,0:T(8,128)(2,1)S(1)} collective-permute-done((bf16[24,64,128]{2,1,0:T(8,128)(2,1)S(1)}, bf16[24,64,128]{2,1,0:T(8,128)(2,1)S(1)}, u32[]{:S(2)}, u32[]{:S(2)}) %collective-permute-start.5) | collective-permute-done | bytes 393248 | tf_op jit(solution)/shard_map/ppermute | solution.py:99
  137.6 0.0 collective-permute-done.2
  137.6 0.0 collective-permute-done.3
  137.6 0.5 fusion.9
  138.2 2.9 %collective-permute-start.7 = (bf16[3,320,128]{2,1,0:T(8,128)(2,1)S(1)}, bf16[3,320,128]{2,1,0:T(8,128)(2,1)S(1)}, u32[]{:S(2)}, u32[]{:S(2)}) collective-permute-start(bf16[3,320,128]{2,1,0:T(8,128)(2,1)S(1)} %pad_maximum_fusion.1), channel_id=1, source_target_pairs={{0,128},{16,144},{32,160},{48,176},{64,192},{80,208},{96,224},{112... | collective-permute-start | bytes 737288 | tf_op jit(solution)/shard_map/ppermute | solution.py:99
  141.1 6.3 %collective-permute-start.6 = (bf16[3,320,128]{2,1,0:T(8,128)(2,1)S(1)}, bf16[3,320,128]{2,1,0:T(8,128)(2,1)S(1)}, u32[]{:S(2)}, u32[]{:S(2)}) collective-permute-start(bf16[3,320,128]{2,1,0:T(8,128)(2,1)S(1)} %pad_maximum_fusion), channel_id=1, source_target_pairs={{0,896},{16,912},{32,928},{48,944},{64,960},{80,976},{96,992},{112... | collective-permute-start | bytes 737288 | tf_op jit(solution)/shard_map/ppermute | solution.py:99
  147.4 4.4 %collective-permute-start.8 = (s32[32,1,128]{2,1,0:T(1,128)S(1)}, s32[32,1,128]{2,1,0:T(1,128)S(1)}, u32[]{:S(2)}, u32[]{:S(2)}) collective-permute-start(s32[32,1,128]{2,1,0:T(1,128)S(1)} %all-to-all-done), channel_id=1, source_target_pairs={{0,16},{16,0},{32,48},{48,32},{64,80},{80,64},{96,112},{112,96},{1... | collective-permute-start | bytes 49160 | tf_op jit(solution)/shard_map/ppermute | solution.py:104
  151.8 0.5 compare_select_fusion.1.codes
  152.3 16.2 %collective-permute-done.7 = bf16[3,320,128]{2,1,0:T(8,128)(2,1)S(1)} collective-permute-done((bf16[3,320,128]{2,1,0:T(8,128)(2,1)S(1)}, bf16[3,320,128]{2,1,0:T(8,128)(2,1)S(1)}, u32[]{:S(2)}, u32[]{:S(2)}) %collective-permute-start.7) | collective-permute-done | bytes 245792 | tf_op jit(solution)/shard_map/ppermute | solution.py:99
  168.6 0.0 collective-permute-done.6
  168.6 0.1 slice_add_fusion
  168.8 5.7 %collective-permute-start.10 = (bf16[3,128,128]{2,1,0:T(8,128)(2,1)S(1)}, bf16[3,128,128]{2,1,0:T(8,128)(2,1)S(1)}, u32[]{:S(2)}, u32[]{:S(2)}) collective-permute-start(bf16[3,128,128]{2,1,0:T(8,128)(2,1)S(1)} %pad_maximum_fusion.3), channel_id=1, source_target_pairs={{0,384},{16,400},{32,416},{48,432},{64,448},{80,464},{96,480},{112... | collective-permute-start | bytes 294920 | tf_op jit(solution)/shard_map/ppermute | solution.py:99
  174.5 13.1 %collective-permute-start.9 = (bf16[3,128,128]{2,1,0:T(8,128)(2,1)S(1)}, bf16[3,128,128]{2,1,0:T(8,128)(2,1)S(1)}, u32[]{:S(2)}, u32[]{:S(2)}) collective-permute-start(bf16[3,128,128]{2,1,0:T(8,128)(2,1)S(1)} %pad_maximum_fusion.2), channel_id=1, source_target_pairs={{0,640},{16,656},{32,672},{48,688},{64,704},{80,720},{96,736},{112... | collective-permute-start | bytes 294920 | tf_op jit(solution)/shard_map/ppermute | solution.py:99
  187.6 0.0 collective-permute-done.8
  187.6 0.1 fusion.8
  187.7 0.7 select_n.25.codes_far
  188.4 20.0 %all-gather.2.cloned.1.call-done.tiles = bf16[192,128,128]{2,1,0:T(8,128)(2,1)} async-done(((bf16[3,128,128]{2,1,0:T(8,128)(2,1)}), bf16[192,128,128]{2,1,0:T(8,128)(2,1)}) %all-gather.2.cloned.1.call-update) | async-done | bytes 6291472 | tf_op jit(solution)/shard_map/all_gather | solution.py:122
  208.4 8.0 %token_grads.1 = (bf16[128,896]{1,0:T(8,128)(2,1)}, bf16[128,896]{1,0:T(8,128)(2,1)}) custom-call(s32[3]{0:T(128)} %copy-done.1, s32[96]{0:T(128)} %compare_select_fusion.1.codes, s32[96]{0:T(128)} %select_n.25.codes_far, bf16[192,128,128]{2,1,0:T(8,128)(2,1)} %all-gather.2.cloned.1.call-done.tiles, bf16[128,4096]{1,0:T(8,128)(2,1)} %bitcast.13, ...), custom_call_target="tpu_custom_call" | custom-call | flops 939524096 | bytes 16777216 | tf_op jit(solution)/shard_map/token_grads/pallas_call | solution.py:191
  216.3 0.0 collective-permute-done.10
  216.4 0.0 collective-permute-done.9
  216.4 0.7 convert_add_fusion.1
  (13 shorter events, 0.3 us)
Async XLA Ops:
  7.2 201.2 %all-gather.2.cloned.1.call-start = ((), (), s32[]{:S(2)}) async-start(), calls=%async_computation.2 | async-start | bytes 6389760 | tf_op jit(solution)/shard_map/all_gather | solution.py:122
  7.9 25.1 %copy-start.4 = (s32[3]{0:T(128)S(1)}, s32[3]{0:T(128)}, u32[]{:S(2)}) copy-start(s32[3]{0:T(128)} %param.11) | copy-start | bytes 40
  7.9 52.9 %copy-start.2 = (bf16[128,896]{1,0:T(8,128)(2,1)S(1)}, bf16[128,896]{1,0:T(8,128)(2,1)}, u32[]{:S(2)}) copy-start(bf16[128,896]{1,0:T(8,128)(2,1)} %gate_ref.1) | copy-start | bytes 688132
  8.9 52.1 %copy-start.3 = (bf16[128,896]{1,0:T(8,128)(2,1)S(1)}, bf16[128,896]{1,0:T(8,128)(2,1)}, u32[]{:S(2)}) copy-start(bf16[128,896]{1,0:T(8,128)(2,1)} %up_ref.1) | copy-start | bytes 688132
  29.0 55.7 %copy-start = (bf16[16,8,4096]{2,1,0:T(8,128)(2,1)}, bf16[16,8,4096]{2,1,0:T(8,128)(2,1)S(1)}, u32[]{:S(2)}) copy-start(bf16[16,8,4096]{2,1,0:T(8,128)(2,1)S(1)} %all_to_all.10) | copy-start | bytes 3145732
  29.0 50.2 %collective-permute-start.1 = (bf16[128,4096]{1,0:T(8,128)(2,1)S(1)}, bf16[128,4096]{1,0:T(8,128)(2,1)S(1)}, u32[]{:S(2)}, u32[]{:S(2)}) collective-permute-start(bf16[128,4096]{1,0:T(8,128)(2,1)S(1)} %bitcast.11), channel_id=1, source_target_pairs={{0,16},{16,0},{32,48},{48,32},{64,80},{80,64},{96,112},{112,96},{1... | collective-permute-start | bytes 3145736 | tf_op jit(solution)/shard_map/ppermute | solution.py:104
  33.6 45.4 %all-to-all-start = ((s32[32,1,128]{2,1,0:T(1,128)}), s32[32,1,128]{2,1,0:T(1,128)S(1)}, u32[]{:S(2)}, u32[]{:S(2)}) async-start(s32[32,1,128]{2,1,0:T(1,128)} %broadcast_in_dim.19), calls=%async_computation | async-start | bytes 32768 | tf_op jit(solution)/shard_map/all_to_all | solution.py:126
  61.3 17.9 %collective-permute-start = (bf16[896,128]{1,0:T(8,128)(2,1)S(1)}, bf16[896,128]{1,0:T(8,128)(2,1)S(1)}, u32[]{:S(2)}, u32[]{:S(2)}) collective-permute-start(bf16[896,128]{1,0:T(8,128)(2,1)S(1)} %fusion.5.hid_a), channel_id=1, source_target_pairs={{0,16},{16,0},{32,48},{48,32},{64,80},{80,64},{96,112},{112,96},{1... | collective-permute-start | bytes 688136 | tf_op jit(solution)/shard_map/ppermute | solution.py:104
  63.9 20.8 %copy-start.1 = (s32[3]{0:T(128)}, s32[3]{0:T(128)S(1)}, u32[]{:S(2)}) copy-start(s32[3]{0:T(128)S(1)} %pad_add_fusion.place) | copy-start | bytes 40
  84.7 52.9 %collective-permute-start.2 = (bf16[24,128,128]{2,1,0:T(8,128)(2,1)S(1)}, bf16[24,128,128]{2,1,0:T(8,128)(2,1)S(1)}, u32[]{:S(2)}, u32[]{:S(2)}) collective-permute-start(bf16[24,128,128]{2,1,0:T(8,128)(2,1)S(1)} %get-tuple-element.29), channel_id=1, source_target_pairs={{0,992},{16,1008},{32,0},{48,16},{64,32},{80,48},{96,64},{112,80},... | collective-permute-start | bytes 2359304 | tf_op jit(solution)/shard_map/ppermute | solution.py:99
  87.6 49.9 %collective-permute-start.3 = (bf16[24,128,128]{2,1,0:T(8,128)(2,1)S(1)}, bf16[24,128,128]{2,1,0:T(8,128)(2,1)S(1)}, u32[]{:S(2)}, u32[]{:S(2)}) collective-permute-start(bf16[24,128,128]{2,1,0:T(8,128)(2,1)S(1)} %get-tuple-element.30), channel_id=1, source_target_pairs={{0,32},{16,48},{32,64},{48,80},{64,96},{80,112},{96,128},{112,144}... | collective-permute-start | bytes 2359304 | tf_op jit(solution)/shard_map/ppermute | solution.py:99
  91.2 32.9 %collective-permute-start.4 = (bf16[24,64,128]{2,1,0:T(8,128)(2,1)S(1)}, bf16[24,64,128]{2,1,0:T(8,128)(2,1)S(1)}, u32[]{:S(2)}, u32[]{:S(2)}) collective-permute-start(bf16[24,64,128]{2,1,0:T(8,128)(2,1)S(1)} %get-tuple-element.31), channel_id=1, source_target_pairs={{0,960},{16,976},{32,992},{48,1008},{64,0},{80,16},{96,32},{112,48... | collective-permute-start | bytes 1179656 | tf_op jit(solution)/shard_map/ppermute | solution.py:99
  94.8 42.8 %collective-permute-start.5 = (bf16[24,64,128]{2,1,0:T(8,128)(2,1)S(1)}, bf16[24,64,128]{2,1,0:T(8,128)(2,1)S(1)}, u32[]{:S(2)}, u32[]{:S(2)}) collective-permute-start(bf16[24,64,128]{2,1,0:T(8,128)(2,1)S(1)} %get-tuple-element.32), channel_id=1, source_target_pairs={{0,64},{16,80},{32,96},{48,112},{64,128},{80,144},{96,160},{112,17... | collective-permute-start | bytes 1179656 | tf_op jit(solution)/shard_map/ppermute | solution.py:99
  138.2 30.3 %collective-permute-start.7 = (bf16[3,320,128]{2,1,0:T(8,128)(2,1)S(1)}, bf16[3,320,128]{2,1,0:T(8,128)(2,1)S(1)}, u32[]{:S(2)}, u32[]{:S(2)}) collective-permute-start(bf16[3,320,128]{2,1,0:T(8,128)(2,1)S(1)} %pad_maximum_fusion.1), channel_id=1, source_target_pairs={{0,128},{16,144},{32,160},{48,176},{64,192},{80,208},{96,224},{112... | collective-permute-start | bytes 737288 | tf_op jit(solution)/shard_map/ppermute | solution.py:99
  141.1 27.5 %collective-permute-start.6 = (bf16[3,320,128]{2,1,0:T(8,128)(2,1)S(1)}, bf16[3,320,128]{2,1,0:T(8,128)(2,1)S(1)}, u32[]{:S(2)}, u32[]{:S(2)}) collective-permute-start(bf16[3,320,128]{2,1,0:T(8,128)(2,1)S(1)} %pad_maximum_fusion), channel_id=1, source_target_pairs={{0,896},{16,912},{32,928},{48,944},{64,960},{80,976},{96,992},{112... | collective-permute-start | bytes 737288 | tf_op jit(solution)/shard_map/ppermute | solution.py:99
  147.4 40.2 %collective-permute-start.8 = (s32[32,1,128]{2,1,0:T(1,128)S(1)}, s32[32,1,128]{2,1,0:T(1,128)S(1)}, u32[]{:S(2)}, u32[]{:S(2)}) collective-permute-start(s32[32,1,128]{2,1,0:T(1,128)S(1)} %all-to-all-done), channel_id=1, source_target_pairs={{0,16},{16,0},{32,48},{48,32},{64,80},{80,64},{96,112},{112,96},{1... | collective-permute-start | bytes 49160 | tf_op jit(solution)/shard_map/ppermute | solution.py:104
  168.8 47.6 %collective-permute-start.10 = (bf16[3,128,128]{2,1,0:T(8,128)(2,1)S(1)}, bf16[3,128,128]{2,1,0:T(8,128)(2,1)S(1)}, u32[]{:S(2)}, u32[]{:S(2)}) collective-permute-start(bf16[3,128,128]{2,1,0:T(8,128)(2,1)S(1)} %pad_maximum_fusion.3), channel_id=1, source_target_pairs={{0,384},{16,400},{32,416},{48,432},{64,448},{80,464},{96,480},{112... | collective-permute-start | bytes 294920 | tf_op jit(solution)/shard_map/ppermute | solution.py:99
  174.5 41.9 %collective-permute-start.9 = (bf16[3,128,128]{2,1,0:T(8,128)(2,1)S(1)}, bf16[3,128,128]{2,1,0:T(8,128)(2,1)S(1)}, u32[]{:S(2)}, u32[]{:S(2)}) collective-permute-start(bf16[3,128,128]{2,1,0:T(8,128)(2,1)S(1)} %pad_maximum_fusion.2), channel_id=1, source_target_pairs={{0,640},{16,656},{32,672},{48,688},{64,704},{80,720},{96,736},{112... | collective-permute-start | bytes 294920 | tf_op jit(solution)/shard_map/ppermute | solution.py:99
Sparse Core Ops, SparseCore 0:
  10.7 197.6 all-gather.1

commit v6 on v3

--- a/solution.py
+++ b/solution.py
@@ -171,19 +171,21 @@
     part = part.reshape(owners // 4, slots, side, side)
 
     half = side // 2
-    down = jnp.concatenate([part[1], part[6], part[4, :, :half]], axis=1).astype(bf16)
-    up = jnp.concatenate([part[7], part[2], part[4, :, half:]], axis=1).astype(bf16)
+    down = jnp.concatenate([part[1], part[3]], axis=1).astype(bf16)
+    up = jnp.concatenate([part[7], part[5]], axis=1).astype(bf16)
+    far_low = shift_z(part[4, :, :half].astype(bf16), -8, owners).astype(f32)
+    far_high = shift_z(part[4, :, half:].astype(bf16), 8, owners).astype(f32)
     down_got = shift_z(down, -4, owners).astype(f32)
     up_got = shift_z(up, 4, owners).astype(f32)
     mine = part[0] + down_got[:, :side] + up_got[:, :side]
-    ahead = part[3] + up_got[:, side : 2 * side]
-    ahead = jnp.concatenate([ahead[:, :half] + down_got[:, 2 * side :], ahead[:, half:]], axis=1)
-    behind = part[5] + down_got[:, side : 2 * side]
-    behind = jnp.concatenate([behind[:, :half], behind[:, half:] + up_got[:, 2 * side :]], axis=1)
+    ahead = part[2] + down_got[:, side:]
+    ahead = jnp.concatenate([ahead[:, :half] + far_low, ahead[:, half:]], axis=1)
+    behind = part[6] + up_got[:, side:]
+    behind = jnp.concatenate([behind[:, :half], behind[:, half:] + far_high], axis=1)
     ahead, behind = ahead.astype(bf16), behind.astype(bf16)
     gathered, codes_far, _, _ = lax.optimization_barrier((gathered, codes_far, ahead, behind))
-    ahead_got = shift_z(ahead, -12, owners).astype(f32)
-    behind_got = shift_z(behind, 12, owners).astype(f32)
+    ahead_got = shift_z(ahead, -8, owners).astype(f32)
+    behind_got = shift_z(behind, 8, owners).astype(f32)
 
     dgate, dup = pl.pallas_call(
         functools.partial(token_kernel, owners, slots, rows_b),

time: 225 us -> 218 us (0.969)
  the two profiles are of different devices: /device:TPU:117 before, /device:TPU:40 now
where the time goes in v6:
time: 218 us; the launch traced here: 217 us
  starting transfers between devices  87.1 us (40%)
  waiting for transfers between devices  74.3 us (34%)
  blocking collectives  22.6 us (10%)
  between operations  14.4 us (7%)
  Pallas kernels  13.9 us (6%)
  local copies, waits for them, and re-layouts  2.85 us (1%)
    ppermute x10, waiting for transfers between devices, shift_z(): return lax.ppermute(value, 'dp', pairs)  54.9 us
    ppermute x10, starting transfers between devices, shift_z(): return lax.ppermute(value, 'dp', pairs)  52.7 us
    all_to_all x1, starting transfers between devices, local(): lax.all_to_all(jnp.broadcast_to(own, (owners, 1, 128)), 'dp', 0, 0, tiled...  28.6 us
    all_to_all x1, blocking collectives, local(): lax.all_to_all(jnp.broadcast_to(cotan[None], (members, tok_dev, width)),...  22.6 us
    all_to_all x1, waiting for transfers between devices, local(): lax.all_to_all(jnp.broadcast_to(own, (owners, 1, 128)), 'dp', 0, 0, tiled...  18.7 us
    pallas_call x1, Pallas kernels, local(): pl.pallas_call(functools.partial(token_kernel, owners, slots, rows_b), ou...  8.4 us
    ppermute x3, starting transfers between devices, swap_core(): return lax.ppermute(value, 'dp', pairs)  5.75 us
    pallas_call x1, Pallas kernels, local(): pl.pallas_call(functools.partial(grad_kernel, owners, slots, rows_b, fact...  5.48 us
  transfers between devices with their start and end apart: 15, of which 6 were waited for; matrix products, arithmetic and copies ran while one was open for 2% of the time, Pallas kernels for 6%

profile of v6, /device:TPU:40, one launch (start us, length us, event | category | flops | bytes accessed | tf_op | source)
XLA Modules:
  0.0 216.9 jit_solution(13456986289686058067)
XLA Ops:
  7.2 0.0 all-gather.2.cloned.1.call-start
  7.2 0.7 all-gather.2.cloned.1.call-update
  7.9 0.0 copy-start.5
  7.9 0.0 copy-start.3
  7.9 1.0 broadcast_in_dim.5
  8.9 0.0 copy-start.4
  8.9 22.6 %all_to_all.10 = bf16[16,8,4096]{2,1,0:T(8,128)(2,1)S(1)} all-to-all(bf16[16,8,4096]{2,1,0:T(8,128)(2,1)S(1)} %broadcast_in_dim.5), channel_id=1, replica_groups=mesh['dp'=64,'tensor'=16] {'tensor'}, dimensions={0} | all-to-all | bytes 2097152 | tf_op jit(solution)/shard_map/all_to_all | solution.py:134
  31.6 0.0 copy-start
  31.6 1.9 collective-permute-start.1
  33.5 0.0 copy-done.5
  33.5 0.6 broadcast_in_dim.4
  34.1 28.6 %all-to-all-start = ((s32[32,1,128]{2,1,0:T(1,128)}), s32[32,1,128]{2,1,0:T(1,128)S(1)}, u32[]{:S(2)}, u32[]{:S(2)}) async-start(s32[32,1,128]{2,1,0:T(1,128)} %broadcast_in_dim.4), calls=%async_computation | async-start | bytes 32768 | tf_op jit(solution)/shard_map/all_to_all | solution.py:127
  62.7 0.0 copy-done.3
  62.7 0.2 copy.12
  62.9 0.0 copy-done.4
  62.9 0.2 copy.13
  63.1 0.1 fusion.5.hid_a
  63.3 1.9 collective-permute-start
  65.2 0.1 pad_add_fusion.place
  65.3 0.0 copy-start.2
  65.3 18.7 %all-to-all-done = s32[32,1,128]{2,1,0:T(1,128)S(1)} async-done(((s32[32,1,128]{2,1,0:T(1,128)}), s32[32,1,128]{2,1,0:T(1,128)S(1)}, u32[]{:S(2)}, u32[]{:S(2)}) %all-to-all-start) | async-done | bytes 16416 | tf_op jit(solution)/shard_map/all_to_all | solution.py:127
  84.0 0.1 reshape_squeeze.6.codes
  84.1 0.0 copy-start.1
  84.1 0.0 collective-permute-done.hid_b
  84.2 0.0 collective-permute-done.1.cot_b
  84.2 5.5 %grad_blocks.1 = (bf16[24,128,128]{2,1,0:T(8,128)(2,1)S(1)}, bf16[24,128,128]{2,1,0:T(8,128)(2,1)S(1)}, bf16[24,64,128]{2,1,0:T(8,128)(2,1)S(1)}, bf16[24,64,128]{2,1,0:T(8,128)(2,1)S(1)}, f32[24,128,128]{2,1,0:T(8,128)S(1)}) custom-call(s32[3]{0:T(128)S(1)} %pad_add_fusion.place, s32[96]{0:T(128)S(1)} %reshape_squeeze.6.codes, ...), custom_call_target="tpu_custom_call" | custom-call | flops 1879048192 | bytes 8388608 | tf_op jit(solution)/shard_map/grad_blocks/pallas_call | solution.py:149
  89.7 0.0 copy-done
  89.7 0.0 copy-done.2
  89.7 0.0 copy-done.1
  89.7 3.4 %collective-permute-start.2 = (bf16[24,128,128]{2,1,0:T(8,128)(2,1)S(1)}, bf16[24,128,128]{2,1,0:T(8,128)(2,1)S(1)}, u32[]{:S(2)}, u32[]{:S(2)}) collective-permute-start(bf16[24,128,128]{2,1,0:T(8,128)(2,1)S(1)} %get-tuple-element.28), channel_id=1, source_target_pairs={{0,992},{16,1008},{32,0},{48,16},{64,32},{80,48},{96,64},{112,80},... | collective-permute-start | bytes 2359304 | tf_op jit(solution)/shard_map/ppermute | solution.py:100
  93.0 2.5 %collective-permute-start.3 = (bf16[24,128,128]{2,1,0:T(8,128)(2,1)S(1)}, bf16[24,128,128]{2,1,0:T(8,128)(2,1)S(1)}, u32[]{:S(2)}, u32[]{:S(2)}) collective-permute-start(bf16[24,128,128]{2,1,0:T(8,128)(2,1)S(1)} %get-tuple-element.29), channel_id=1, source_target_pairs={{0,32},{16,48},{32,64},{48,80},{64,96},{80,112},{96,128},{112,144}... | collective-permute-start | bytes 2359304 | tf_op jit(solution)/shard_map/ppermute | solution.py:100
  95.5 4.3 %collective-permute-start.4 = (bf16[24,64,128]{2,1,0:T(8,128)(2,1)S(1)}, bf16[24,64,128]{2,1,0:T(8,128)(2,1)S(1)}, u32[]{:S(2)}, u32[]{:S(2)}) collective-permute-start(bf16[24,64,128]{2,1,0:T(8,128)(2,1)S(1)} %get-tuple-element.30), channel_id=1, source_target_pairs={{0,960},{16,976},{32,992},{48,1008},{64,0},{80,16},{96,32},{112,48... | collective-permute-start | bytes 1179656 | tf_op jit(solution)/shard_map/ppermute | solution.py:100
  99.8 2.5 %collective-permute-start.5 = (bf16[24,64,128]{2,1,0:T(8,128)(2,1)S(1)}, bf16[24,64,128]{2,1,0:T(8,128)(2,1)S(1)}, u32[]{:S(2)}, u32[]{:S(2)}) collective-permute-start(bf16[24,64,128]{2,1,0:T(8,128)(2,1)S(1)} %get-tuple-element.31), channel_id=1, source_target_pairs={{0,64},{16,80},{32,96},{48,112},{64,128},{80,144},{96,160},{112,17... | collective-permute-start | bytes 1179656 | tf_op jit(solution)/shard_map/ppermute | solution.py:100
  102.3 1.9 collective-permute-start.8
  104.2 27.0 %collective-permute-done.4 = bf16[24,64,128]{2,1,0:T(8,128)(2,1)S(1)} collective-permute-done((bf16[24,64,128]{2,1,0:T(8,128)(2,1)S(1)}, bf16[24,64,128]{2,1,0:T(8,128)(2,1)S(1)}, u32[]{:S(2)}, u32[]{:S(2)}) %collective-permute-start.4) | collective-permute-done | bytes 393248 | tf_op jit(solution)/shard_map/ppermute | solution.py:100
  131.2 10.9 %collective-permute-done.5 = bf16[24,64,128]{2,1,0:T(8,128)(2,1)S(1)} collective-permute-done((bf16[24,64,128]{2,1,0:T(8,128)(2,1)S(1)}, bf16[24,64,128]{2,1,0:T(8,128)(2,1)S(1)}, u32[]{:S(2)}, u32[]{:S(2)}) %collective-permute-start.5) | collective-permute-done | bytes 393248 | tf_op jit(solution)/shard_map/ppermute | solution.py:100
  142.1 0.0 collective-permute-done.2
  142.1 0.0 collective-permute-done.3
  142.2 0.5 fusion.8
  142.7 3.6 %collective-permute-start.6 = (bf16[3,256,128]{2,1,0:T(8,128)(2,1)S(1)}, bf16[3,256,128]{2,1,0:T(8,128)(2,1)S(1)}, u32[]{:S(2)}, u32[]{:S(2)}) collective-permute-start(bf16[3,256,128]{2,1,0:T(8,128)(2,1)S(1)} %pad_maximum_fusion), channel_id=1, source_target_pairs={{0,896},{16,912},{32,928},{48,944},{64,960},{80,976},{96,992},{112... | collective-permute-start | bytes 589832 | tf_op jit(solution)/shard_map/ppermute | solution.py:100
  146.3 6.2 %collective-permute-start.7 = (bf16[3,256,128]{2,1,0:T(8,128)(2,1)S(1)}, bf16[3,256,128]{2,1,0:T(8,128)(2,1)S(1)}, u32[]{:S(2)}, u32[]{:S(2)}) collective-permute-start(bf16[3,256,128]{2,1,0:T(8,128)(2,1)S(1)} %pad_maximum_fusion.1), channel_id=1, source_target_pairs={{0,128},{16,144},{32,160},{48,176},{64,192},{80,208},{96,224},{112... | collective-permute-start | bytes 589832 | tf_op jit(solution)/shard_map/ppermute | solution.py:100
  152.5 6.2 %collective-permute-start.10 = (bf16[3,64,128]{2,1,0:T(8,128)(2,1)S(1)}, bf16[3,64,128]{2,1,0:T(8,128)(2,1)S(1)}, u32[]{:S(2)}, u32[]{:S(2)}) collective-permute-start(bf16[3,64,128]{2,1,0:T(8,128)(2,1)S(1)} %get-tuple-element.44), channel_id=1, source_target_pairs={{0,256},{16,272},{32,288},{48,304},{64,320},{80,336},{96,352},{112... | collective-permute-start | bytes 147464 | tf_op jit(solution)/shard_map/ppermute | solution.py:100
  158.7 8.4 %collective-permute-start.9 = (bf16[3,64,128]{2,1,0:T(8,128)(2,1)S(1)}, bf16[3,64,128]{2,1,0:T(8,128)(2,1)S(1)}, u32[]{:S(2)}, u32[]{:S(2)}) collective-permute-start(bf16[3,64,128]{2,1,0:T(8,128)(2,1)S(1)} %get-tuple-element.45), channel_id=1, source_target_pairs={{0,768},{16,784},{32,800},{48,816},{64,832},{80,848},{96,864},{112... | collective-permute-start | bytes 147464 | tf_op jit(solution)/shard_map/ppermute | solution.py:100
  167.1 5.8 %collective-permute-done.6 = bf16[3,256,128]{2,1,0:T(8,128)(2,1)S(1)} collective-permute-done((bf16[3,256,128]{2,1,0:T(8,128)(2,1)S(1)}, bf16[3,256,128]{2,1,0:T(8,128)(2,1)S(1)}, u32[]{:S(2)}, u32[]{:S(2)}) %collective-permute-start.6) | collective-permute-done | bytes 196640 | tf_op jit(solution)/shard_map/ppermute | solution.py:100
  172.9 0.0 collective-permute-done.7
  172.9 0.1 slice_add_fusion
  173.0 4.9 %collective-permute-done.10 = bf16[3,64,128]{2,1,0:T(8,128)(2,1)S(1)} collective-permute-done((bf16[3,64,128]{2,1,0:T(8,128)(2,1)S(1)}, bf16[3,64,128]{2,1,0:T(8,128)(2,1)S(1)}, u32[]{:S(2)}, u32[]{:S(2)}) %collective-permute-start.10) | collective-permute-done | bytes 49184 | tf_op jit(solution)/shard_map/ppermute | solution.py:100
  178.0 13.9 %collective-permute-start.12 = (bf16[3,128,128]{2,1,0:T(8,128)(2,1)S(1)}, bf16[3,128,128]{2,1,0:T(8,128)(2,1)S(1)}, u32[]{:S(2)}, u32[]{:S(2)}) collective-permute-start(bf16[3,128,128]{2,1,0:T(8,128)(2,1)S(1)} %pad_maximum_fusion.3), channel_id=1, source_target_pairs={{0,256},{16,272},{32,288},{48,304},{64,320},{80,336},{96,352},{112... | collective-permute-start | bytes 294920 | tf_op jit(solution)/shard_map/ppermute | solution.py:100
  191.9 0.0 collective-permute-done.9
  191.9 1.9 collective-permute-start.11
  193.9 0.0 collective-permute-done.8
  193.9 0.6 reshape_squeeze.7.codes_far
  194.6 0.0 all-gather.2.cloned.1.call-done.tiles
  194.6 8.4 %token_grads.1 = (bf16[128,896]{1,0:T(8,128)(2,1)}, bf16[128,896]{1,0:T(8,128)(2,1)}) custom-call(s32[3]{0:T(128)} %copy-done.2, s32[96]{0:T(128)} %copy-done.1, s32[96]{0:T(128)} %reshape_squeeze.7.codes_far, bf16[192,128,128]{2,1,0:T(8,128)(2,1)} %all-gather.2.cloned.1.call-done.tiles, bf16[128,4096]{1,0:T(8,128)(2,1)} %bitcast.13, ...), custom_call_target="tpu_custom_call" | custom-call | flops 939524096 | bytes 16777216 | tf_op jit(solution)/shard_map/token_grads/pallas_call | solution.py:190
  203.0 0.0 collective-permute-done.12
  203.0 6.3 %collective-permute-done.11 = bf16[3,128,128]{2,1,0:T(8,128)(2,1)S(1)} collective-permute-done((bf16[3,128,128]{2,1,0:T(8,128)(2,1)S(1)}, bf16[3,128,128]{2,1,0:T(8,128)(2,1)S(1)}, u32[]{:S(2)}, u32[]{:S(2)}) %collective-permute-start.11) | collective-permute-done | bytes 98336 | tf_op jit(solution)/shard_map/ppermute | solution.py:100
  209.3 0.7 convert_add_fusion.1
  (15 shorter events, 0.3 us)
Async XLA Ops:
  7.2 187.4 %all-gather.2.cloned.1.call-start = ((), (), s32[]{:S(2)}) async-start(), calls=%async_computation.2 | async-start | bytes 6389760 | tf_op jit(solution)/shard_map/all_gather | solution.py:123
  7.9 25.6 %copy-start.5 = (s32[3]{0:T(128)S(1)}, s32[3]{0:T(128)}, u32[]{:S(2)}) copy-start(s32[3]{0:T(128)} %param.11) | copy-start | bytes 40
  7.9 54.8 %copy-start.3 = (bf16[128,896]{1,0:T(8,128)(2,1)S(1)}, bf16[128,896]{1,0:T(8,128)(2,1)}, u32[]{:S(2)}) copy-start(bf16[128,896]{1,0:T(8,128)(2,1)} %gate_ref.1) | copy-start | bytes 688132
  8.9 54.0 %copy-start.4 = (bf16[128,896]{1,0:T(8,128)(2,1)S(1)}, bf16[128,896]{1,0:T(8,128)(2,1)}, u32[]{:S(2)}) copy-start(bf16[128,896]{1,0:T(8,128)(2,1)} %up_ref.1) | copy-start | bytes 688132
  31.6 58.1 %copy-start = (bf16[16,8,4096]{2,1,0:T(8,128)(2,1)}, bf16[16,8,4096]{2,1,0:T(8,128)(2,1)S(1)}, u32[]{:S(2)}) copy-start(bf16[16,8,4096]{2,1,0:T(8,128)(2,1)S(1)} %all_to_all.10) | copy-start | bytes 3145732
  31.6 52.6 %collective-permute-start.1 = (bf16[128,4096]{1,0:T(8,128)(2,1)S(1)}, bf16[128,4096]{1,0:T(8,128)(2,1)S(1)}, u32[]{:S(2)}, u32[]{:S(2)}) collective-permute-start(bf16[128,4096]{1,0:T(8,128)(2,1)S(1)} %bitcast.11), channel_id=1, source_target_pairs={{0,16},{16,0},{32,48},{48,32},{64,80},{80,64},{96,112},{112,96},{1... | collective-permute-start | bytes 3145736 | tf_op jit(solution)/shard_map/ppermute | solution.py:105
  34.1 49.9 %all-to-all-start = ((s32[32,1,128]{2,1,0:T(1,128)}), s32[32,1,128]{2,1,0:T(1,128)S(1)}, u32[]{:S(2)}, u32[]{:S(2)}) async-start(s32[32,1,128]{2,1,0:T(1,128)} %broadcast_in_dim.4), calls=%async_computation | async-start | bytes 32768 | tf_op jit(solution)/shard_map/all_to_all | solution.py:127
  63.3 20.9 %collective-permute-start = (bf16[896,128]{1,0:T(8,128)(2,1)S(1)}, bf16[896,128]{1,0:T(8,128)(2,1)S(1)}, u32[]{:S(2)}, u32[]{:S(2)}) collective-permute-start(bf16[896,128]{1,0:T(8,128)(2,1)S(1)} %fusion.5.hid_a), channel_id=1, source_target_pairs={{0,16},{16,0},{32,48},{48,32},{64,80},{80,64},{96,112},{112,96},{1... | collective-permute-start | bytes 688136 | tf_op jit(solution)/shard_map/ppermute | solution.py:105
  65.3 24.4 %copy-start.2 = (s32[3]{0:T(128)}, s32[3]{0:T(128)S(1)}, u32[]{:S(2)}) copy-start(s32[3]{0:T(128)S(1)} %pad_add_fusion.place) | copy-start | bytes 40
  84.1 5.5 %copy-start.1 = (s32[96]{0:T(128)}, s32[96]{0:T(128)S(1)}, u32[]{:S(2)}) copy-start(s32[96]{0:T(128)S(1)} %reshape_squeeze.6.codes) | copy-start | bytes 1156
  89.7 52.5 %collective-permute-start.2 = (bf16[24,128,128]{2,1,0:T(8,128)(2,1)S(1)}, bf16[24,128,128]{2,1,0:T(8,128)(2,1)S(1)}, u32[]{:S(2)}, u32[]{:S(2)}) collective-permute-start(bf16[24,128,128]{2,1,0:T(8,128)(2,1)S(1)} %get-tuple-element.28), channel_id=1, source_target_pairs={{0,992},{16,1008},{32,0},{48,16},{64,32},{80,48},{96,64},{112,80},... | collective-permute-start | bytes 2359304 | tf_op jit(solution)/shard_map/ppermute | solution.py:100
  93.0 49.1 %collective-permute-start.3 = (bf16[24,128,128]{2,1,0:T(8,128)(2,1)S(1)}, bf16[24,128,128]{2,1,0:T(8,128)(2,1)S(1)}, u32[]{:S(2)}, u32[]{:S(2)}) collective-permute-start(bf16[24,128,128]{2,1,0:T(8,128)(2,1)S(1)} %get-tuple-element.29), channel_id=1, source_target_pairs={{0,32},{16,48},{32,64},{48,80},{64,96},{80,112},{96,128},{112,144}... | collective-permute-start | bytes 2359304 | tf_op jit(solution)/shard_map/ppermute | solution.py:100
  95.5 35.7 %collective-permute-start.4 = (bf16[24,64,128]{2,1,0:T(8,128)(2,1)S(1)}, bf16[24,64,128]{2,1,0:T(8,128)(2,1)S(1)}, u32[]{:S(2)}, u32[]{:S(2)}) collective-permute-start(bf16[24,64,128]{2,1,0:T(8,128)(2,1)S(1)} %get-tuple-element.30), channel_id=1, source_target_pairs={{0,960},{16,976},{32,992},{48,1008},{64,0},{80,16},{96,32},{112,48... | collective-permute-start | bytes 1179656 | tf_op jit(solution)/shard_map/ppermute | solution.py:100
  99.8 42.3 %collective-permute-start.5 = (bf16[24,64,128]{2,1,0:T(8,128)(2,1)S(1)}, bf16[24,64,128]{2,1,0:T(8,128)(2,1)S(1)}, u32[]{:S(2)}, u32[]{:S(2)}) collective-permute-start(bf16[24,64,128]{2,1,0:T(8,128)(2,1)S(1)} %get-tuple-element.31), channel_id=1, source_target_pairs={{0,64},{16,80},{32,96},{48,112},{64,128},{80,144},{96,160},{112,17... | collective-permute-start | bytes 1179656 | tf_op jit(solution)/shard_map/ppermute | solution.py:100
  102.3 91.6 %collective-permute-start.8 = (s32[32,1,128]{2,1,0:T(1,128)S(1)}, s32[32,1,128]{2,1,0:T(1,128)S(1)}, u32[]{:S(2)}, u32[]{:S(2)}) collective-permute-start(s32[32,1,128]{2,1,0:T(1,128)S(1)} %all-to-all-done), channel_id=1, source_target_pairs={{0,16},{16,0},{32,48},{48,32},{64,80},{80,64},{96,112},{112,96},{1... | collective-permute-start | bytes 49160 | tf_op jit(solution)/shard_map/ppermute | solution.py:105
  142.7 30.1 %collective-permute-start.6 = (bf16[3,256,128]{2,1,0:T(8,128)(2,1)S(1)}, bf16[3,256,128]{2,1,0:T(8,128)(2,1)S(1)}, u32[]{:S(2)}, u32[]{:S(2)}) collective-permute-start(bf16[3,256,128]{2,1,0:T(8,128)(2,1)S(1)} %pad_maximum_fusion), channel_id=1, source_target_pairs={{0,896},{16,912},{32,928},{48,944},{64,960},{80,976},{96,992},{112... | collective-permute-start | bytes 589832 | tf_op jit(solution)/shard_map/ppermute | solution.py:100
  146.3 26.5 %collective-permute-start.7 = (bf16[3,256,128]{2,1,0:T(8,128)(2,1)S(1)}, bf16[3,256,128]{2,1,0:T(8,128)(2,1)S(1)}, u32[]{:S(2)}, u32[]{:S(2)}) collective-permute-start(bf16[3,256,128]{2,1,0:T(8,128)(2,1)S(1)} %pad_maximum_fusion.1), channel_id=1, source_target_pairs={{0,128},{16,144},{32,160},{48,176},{64,192},{80,208},{96,224},{112... | collective-permute-start | bytes 589832 | tf_op jit(solution)/shard_map/ppermute | solution.py:100
  152.5 25.4 %collective-permute-start.10 = (bf16[3,64,128]{2,1,0:T(8,128)(2,1)S(1)}, bf16[3,64,128]{2,1,0:T(8,128)(2,1)S(1)}, u32[]{:S(2)}, u32[]{:S(2)}) collective-permute-start(bf16[3,64,128]{2,1,0:T(8,128)(2,1)S(1)} %get-tuple-element.44), channel_id=1, source_target_pairs={{0,256},{16,272},{32,288},{48,304},{64,320},{80,336},{96,352},{112... | collective-permute-start | bytes 147464 | tf_op jit(solution)/shard_map/ppermute | solution.py:100
  158.7 33.2 %collective-permute-start.9 = (bf16[3,64,128]{2,1,0:T(8,128)(2,1)S(1)}, bf16[3,64,128]{2,1,0:T(8,128)(2,1)S(1)}, u32[]{:S(2)}, u32[]{:S(2)}) collective-permute-start(bf16[3,64,128]{2,1,0:T(8,128)(2,1)S(1)} %get-tuple-element.45), channel_id=1, source_target_pairs={{0,768},{16,784},{32,800},{48,816},{64,832},{80,848},{96,864},{112... | collective-permute-start | bytes 147464 | tf_op jit(solution)/shard_map/ppermute | solution.py:100
  178.0 25.0 %collective-permute-start.12 = (bf16[3,128,128]{2,1,0:T(8,128)(2,1)S(1)}, bf16[3,128,128]{2,1,0:T(8,128)(2,1)S(1)}, u32[]{:S(2)}, u32[]{:S(2)}) collective-permute-start(bf16[3,128,128]{2,1,0:T(8,128)(2,1)S(1)} %pad_maximum_fusion.3), channel_id=1, source_target_pairs={{0,256},{16,272},{32,288},{48,304},{64,320},{80,336},{96,352},{112... | collective-permute-start | bytes 294920 | tf_op jit(solution)/shard_map/ppermute | solution.py:100
  191.9 17.4 %collective-permute-start.11 = (bf16[3,128,128]{2,1,0:T(8,128)(2,1)S(1)}, bf16[3,128,128]{2,1,0:T(8,128)(2,1)S(1)}, u32[]{:S(2)}, u32[]{:S(2)}) collective-permute-start(bf16[3,128,128]{2,1,0:T(8,128)(2,1)S(1)} %pad_maximum_fusion.2), channel_id=1, source_target_pairs={{0,768},{16,784},{32,800},{48,816},{64,832},{80,848},{96,864},{112... | collective-permute-start | bytes 294920 | tf_op jit(solution)/shard_map/ppermute | solution.py:100
Sparse Core Ops, SparseCore 0:
  10.7 173.0 all-gather.1
